TPU v7x, 32 devices: a whole 2x2x4 slice. The times are simulated.
32 devices in a mesh: seq: 4 (over y, x), batch: 8 (over z, core).
Axes of the slice: x: 2, y: 2, z: 4, core: 2. Of those that a mesh axis runs over, the one named last changes fastest.
Arguments:
- tokens: bfloat16 [32, 1024, 512], P('batch', 'seq'), may hold values from -6 to 6
- lengths: int32 [32], P('batch'), may hold values from 513 to 1024, as said below
- query_weight: bfloat16 [512, 512], replicated, may hold values from -0.25 to 0.25
- key_weight: bfloat16 [512, 512], replicated, may hold values from -0.25 to 0.25
- value_weight: bfloat16 [512, 512], replicated, may hold values from -0.25 to 0.25
- output_weight: bfloat16 [512, 512], replicated, may hold values from -1 to 1
- up_weight: bfloat16 [512, 2048], replicated, may hold values from -0.25 to 0.25
- down_weight: bfloat16 [2048, 512], replicated, may hold values from -0.125 to 0.125
- query_bias: float32 [512], replicated, may hold values from -3 to 3
- value_bias: float32 [512], replicated, may hold values from -3 to 3
- output_bias: float32 [512], replicated, may hold values from -1.75 to 1.75
- up_bias: float32 [2048], replicated, may hold values from -3 to 3
- down_bias: float32 [512], replicated, may hold values from -1.75 to 1.75
- first_gain: float32 [512], replicated, may hold values from 0.25 to 1.75
- first_shift: float32 [512], replicated, may hold values from -1.75 to 1.75
- second_gain: float32 [512], replicated, may hold values from 0.25 to 1.75
- second_shift: float32 [512], replicated, may hold values from -1.75 to 1.75
- cotangent: bfloat16 [32, 1024, 512], P('batch', 'seq'), may hold values from -6 to 6
Outputs:
- layer_out: bfloat16 [32, 1024, 512], P('batch', 'seq')
- input_grad: float32 [32, 1024, 512], P('batch', 'seq')
- grad_query_weight: float32 [512, 512], replicated
- grad_key_weight: float32 [512, 512], replicated
- grad_value_weight: float32 [512, 512], replicated
- grad_output_weight: float32 [512, 512], replicated
- grad_up_weight: float32 [512, 2048], replicated
- grad_down_weight: float32 [2048, 512], replicated
- grad_query_bias: float32 [512], replicated
- grad_value_bias: float32 [512], replicated
- grad_output_bias: float32 [512], replicated
- grad_up_bias: float32 [2048], replicated
- grad_down_bias: float32 [512], replicated
- grad_first_gain: float32 [512], replicated
- grad_first_shift: float32 [512], replicated
- grad_second_gain: float32 [512], replicated
- grad_second_shift: float32 [512], replicated
Inputs may be any that keep to these rules, and one draw needn't show every extreme that they name: `lengths`: among the 4 sequences held by one index of batch, one has length 1024.
All inputs are finite; a program needn't handle non-finite values.
Results may differ from a plain program's by a relative error of at most 0.02.
Values sent between devices are 32-bit elements; how exact they have to be, the bound alone decides.
No kernel may reach another device: no remote copies, remote signals or barrier semaphores. Data moves between devices by JAX's collectives and lax.ppermute only.
A program may use at most 256 MiB of HBM per device.

v0:
```python
import functools
import math

import jax
import jax.numpy as jnp
from jax import lax
from jax.sharding import PartitionSpec as P

HEADS = 8
BLOCK = 16


HIGHEST = lax.Precision.HIGHEST
MASKED = -1e30
EPSILON = 1e-05


def layer_norm(values, gain, shift):
    center = values - jnp.mean(values, axis=-1, keepdims=True)
    variance = jnp.mean(center * center, axis=-1, keepdims=True)
    return center * lax.rsqrt(variance + EPSILON) * gain + shift


def gelu_tanh(values):
    return jax.nn.gelu(values, approximate=True)


def matmul(left, right):
    return jnp.dot(left, right, preferred_element_type=jnp.float32)


def row_product(left, right):
    return lax.dot_general(
        left, right, (((0,), (0,)), ((), ())), preferred_element_type=jnp.float32
    )


def back_product(grads, weight):
    return lax.dot_general(
        grads, weight, (((1,), (1,)), ((), ())), preferred_element_type=jnp.float32
    )


def own_blocks(array):
    return array.reshape((array.shape[0], array.shape[1] // BLOCK, BLOCK) + array.shape[2:])


def sibling_blocks(array):
    paired = array.reshape(
        (array.shape[0], array.shape[1] // (2 * BLOCK), 2, BLOCK) + array.shape[2:]
    )
    return paired[:, :, ::-1].reshape(
        (array.shape[0], array.shape[1] // BLOCK, BLOCK) + array.shape[2:]
    )


def flatten_blocks(array):
    return array.reshape((array.shape[0], array.shape[1] * array.shape[2]) + array.shape[3:])


def spread_rows(array, factor):
    leading = array.shape[:2]
    widened = jnp.broadcast_to(array[:, :, None], leading + (factor,) + array.shape[2:])
    return widened.reshape((leading[0], leading[1] * factor) + array.shape[2:])


def collapse_rows(array, factor):
    return jnp.sum(
        array.reshape((array.shape[0], array.shape[1] // factor, factor) + array.shape[2:]), axis=2
    )


def pool_pairs(array):
    return collapse_rows(array, 2)


def add_at(base, piece, start):
    current = lax.dynamic_slice_in_dim(base, start, piece.shape[1], 1)
    return lax.dynamic_update_slice_in_dim(base, current + piece, start, 1)


def coarse_attend(query_sums, key_sums, value_sums, key_counts, factor):
    head_dim = query_sums.shape[-1] // HEADS
    floored = jnp.maximum(key_counts, 1.0)
    query_means = (query_sums / factor).reshape(query_sums.shape[:-1] + (HEADS, head_dim))
    key_means = (key_sums / floored[..., None]).reshape(key_sums.shape[:-1] + (HEADS, head_dim))
    value_means = (value_sums / floored[..., None]).reshape(
        value_sums.shape[:-1] + (HEADS, head_dim)
    )
    bias_terms = jnp.where(key_counts > 0, jnp.log(floored), MASKED)
    logits = jnp.einsum("sbqhd,sbkhd->sbqhk", query_means, key_means, precision=HIGHEST) * (
        1.0 / math.sqrt(head_dim)
    )
    logits = logits + bias_terms[:, :, None, None, :]
    maxima = jnp.max(logits, axis=-1)
    powers = jnp.exp(logits - maxima[..., None])
    numerators = jnp.einsum("sbqhk,sbkhd->sbqhd", powers, value_means, precision=HIGHEST)
    return (maxima, jnp.sum(powers, axis=-1), numerators)


def cross_level(mine, theirs, their_counts, offset, width_here, factor):
    query_sums = lax.dynamic_slice_in_dim(mine[:, :, 0], offset, width_here, 1)[:, None]

    def cross_attend(query_part, key_part, value_part):
        return coarse_attend(query_part, key_part, value_part, their_counts[:, None], factor)

    return jax.vjp(cross_attend, query_sums, theirs[:, None, :, 1], theirs[:, None, :, 2])


def level_grads(record, biggest, grad_numerator, grad_denominator):
    maxima, totals, numerators, factor = record
    weight = jnp.exp(spread_rows(maxima, factor) - biggest)
    grad_numer = collapse_rows(weight[..., None] * grad_numerator, factor)
    grad_totals = collapse_rows(weight * grad_denominator, factor)
    grad_maxima = jnp.sum(grad_numer * numerators, axis=-1) + grad_totals * totals
    return (grad_maxima, grad_totals, grad_numer)


def local(
    tokens,
    lengths,
    query_weight,
    key_weight,
    value_weight,
    output_weight,
    up_weight,
    down_weight,
    query_bias,
    value_bias,
    output_bias,
    up_bias,
    down_bias,
    first_gain,
    first_shift,
    second_gain,
    second_shift,
    cotangent,
):
    seq_count, tok_count, width = tokens.shape
    head_dim = width // HEADS
    inverse_root = 1.0 / math.sqrt(head_dim)
    row_count = seq_count * tok_count
    shards = lax.axis_size("seq")
    shard_index = lax.axis_index("seq")
    tree_depth = shards.bit_length() - 1
    local_depth = (tok_count // BLOCK).bit_length() - 1
    positions = shard_index * tok_count + jnp.arange(tok_count, dtype=jnp.int32)
    valid_mask = (positions[None, :] < lengths[:, None]).astype(jnp.float32)
    inputs = tokens.astype(jnp.float32)
    normed, norm_pull = jax.vjp(layer_norm, inputs, first_gain, first_shift)
    normed_low = normed.astype(jnp.bfloat16).reshape(row_count, width)
    queries = (matmul(normed_low, query_weight) + query_bias).astype(jnp.bfloat16)
    key_rows = matmul(normed_low, key_weight).astype(jnp.bfloat16)
    value_rows = (matmul(normed_low, value_weight) + value_bias).astype(jnp.bfloat16)
    head_shape = (seq_count, tok_count, HEADS, head_dim)
    query_heads = queries.reshape(head_shape)
    key_heads = key_rows.reshape(head_shape)
    value_heads = value_rows.reshape(head_shape)
    fine_bias = jnp.where(valid_mask > 0, 0.0, MASKED)
    near_keys = jnp.concatenate([own_blocks(key_heads), sibling_blocks(key_heads)], axis=2)
    near_values = jnp.concatenate([own_blocks(value_heads), sibling_blocks(value_heads)], axis=2)
    near_bias = jnp.concatenate([own_blocks(fine_bias), sibling_blocks(fine_bias)], axis=2)
    query_blocks = own_blocks(query_heads)
    logits = (
        jnp.einsum(
            "sbqhd,sbkhd->sbqhk", query_blocks, near_keys, preferred_element_type=jnp.float32
        )
        * inverse_root
    )
    logits = logits + near_bias[:, :, None, None, :]
    fine_maxima = jnp.max(logits, axis=-1)
    fine_powers = jnp.exp(logits - fine_maxima[..., None])
    fine_totals = jnp.sum(fine_powers, axis=-1)
    fine_probs = fine_powers.astype(jnp.bfloat16)
    fine_numer = jnp.einsum(
        "sbqhk,sbkhd->sbqhd", fine_probs, near_values, preferred_element_type=jnp.float32
    )
    levels = [
        (flatten_blocks(fine_maxima), flatten_blocks(fine_totals), flatten_blocks(fine_numer), 1)
    ]
    stacked = jnp.stack(
        [
            queries.astype(jnp.float32).reshape(seq_count, tok_count, width),
            key_rows.astype(jnp.float32).reshape(seq_count, tok_count, width)
            * valid_mask[..., None],
            value_rows.astype(jnp.float32).reshape(seq_count, tok_count, width)
            * valid_mask[..., None],
        ],
        axis=2,
    )
    stacked = pool_pairs(stacked)
    counts = pool_pairs(valid_mask)
    factor = 2
    local_pulls = []
    for level_index in range(1, local_depth):

        def body_attend(
            query_part, key_part, value_part, key_counts=sibling_blocks(counts), scale_factor=factor
        ):
            return coarse_attend(query_part, key_part, value_part, key_counts, scale_factor)

        outputs, pullback = jax.vjp(
            body_attend,
            own_blocks(stacked[:, :, 0]),
            sibling_blocks(stacked[:, :, 1]),
            sibling_blocks(stacked[:, :, 2]),
        )
        levels.append(
            (
                flatten_blocks(outputs[0]),
                flatten_blocks(outputs[1]),
                flatten_blocks(outputs[2]),
                factor,
            )
        )
        local_pulls.append(pullback)
        stacked = pool_pairs(stacked)
        counts = pool_pairs(counts)
        factor = factor * 2
    cross_pulls = []
    pyramid, pyramid_counts = (
        lax.all_gather(stacked, "seq", axis=1, tiled=True),
        lax.all_gather(counts, "seq", axis=1, tiled=True),
    )
    for height in range(tree_depth):
        group = shard_index >> height
        width_here = BLOCK >> height
        offset = shard_index % (1 << height) * width_here
        mine = lax.dynamic_slice_in_dim(pyramid, group * BLOCK, BLOCK, 1)
        theirs = lax.dynamic_slice_in_dim(pyramid, (group ^ 1) * BLOCK, BLOCK, 1)
        their_counts = lax.dynamic_slice_in_dim(pyramid_counts, (group ^ 1) * BLOCK, BLOCK, 1)
        outputs, pullback = cross_level(mine, theirs, their_counts, offset, width_here, factor)
        levels.append(
            (
                outputs[0].reshape(seq_count, width_here, HEADS),
                outputs[1].reshape(seq_count, width_here, HEADS),
                outputs[2].reshape(seq_count, width_here, HEADS, head_dim),
                factor,
            )
        )
        cross_pulls.append((pullback, offset, width_here, group))
        pyramid = pool_pairs(pyramid)
        pyramid_counts = pool_pairs(pyramid_counts)
        factor = factor * 2
    biggest = functools.reduce(
        jnp.maximum, [spread_rows(record[0], record[3]) for record in levels]
    )
    denominator = jnp.zeros((seq_count, tok_count, HEADS), jnp.float32)
    numerator = jnp.zeros((seq_count, tok_count, HEADS, head_dim), jnp.float32)
    for record in levels:
        weight = jnp.exp(spread_rows(record[0], record[3]) - biggest)
        denominator = denominator + weight * spread_rows(record[1], record[3])
        numerator = numerator + weight[..., None] * spread_rows(record[2], record[3])
    attended = numerator / denominator[..., None]
    attended_low = attended.reshape(row_count, width).astype(jnp.bfloat16)
    middle = inputs.reshape(row_count, width) + matmul(attended_low, output_weight) + output_bias
    second, second_pull = jax.vjp(layer_norm, middle, second_gain, second_shift)
    second_low = second.astype(jnp.bfloat16)
    hidden, gelu_pull = jax.vjp(gelu_tanh, matmul(second_low, up_weight) + up_bias)
    hidden_low = hidden.astype(jnp.bfloat16)
    result = middle + matmul(hidden_low, down_weight) + down_bias
    layer_out = result.astype(jnp.bfloat16).reshape(seq_count, tok_count, width)
    grad_result = cotangent.reshape(row_count, width)
    grad_down_weight = row_product(hidden_low, grad_result)
    grad_down_bias = jnp.sum(grad_result.astype(jnp.float32), axis=0)
    grad_hidden = gelu_pull(back_product(grad_result, down_weight))[0].astype(jnp.bfloat16)
    grad_up_weight = row_product(second_low, grad_hidden)
    grad_up_bias = jnp.sum(grad_hidden.astype(jnp.float32), axis=0)
    grad_middle_norm, grad_second_gain, grad_second_shift = second_pull(
        back_product(grad_hidden, up_weight)
    )
    grad_middle = grad_result.astype(jnp.float32) + grad_middle_norm
    grad_project = grad_middle.astype(jnp.bfloat16)
    grad_output_weight = row_product(attended_low, grad_project)
    grad_output_bias = jnp.sum(grad_project.astype(jnp.float32), axis=0)
    grad_attended = (
        back_product(grad_project, output_weight).astype(jnp.bfloat16).astype(jnp.float32)
    )
    grad_attended = grad_attended.reshape(seq_count, tok_count, HEADS, head_dim)
    grad_numerator = grad_attended / denominator[..., None]
    grad_denominator = -jnp.sum(grad_attended * attended, axis=-1) / denominator
    level_cots = [
        level_grads(record, biggest, grad_numerator, grad_denominator) for record in levels
    ]
    grad_fine_numer = own_blocks(level_cots[0][2]).astype(jnp.bfloat16)
    grad_fine_totals = own_blocks(level_cots[0][1])
    grad_probs = jnp.einsum(
        "sbqhd,sbkhd->sbqhk", grad_fine_numer, near_values, preferred_element_type=jnp.float32
    )
    grad_logits = (fine_powers * (grad_probs + grad_fine_totals[..., None])).astype(jnp.bfloat16)
    grad_query_fine = (
        flatten_blocks(
            jnp.einsum(
                "sbqhk,sbkhd->sbqhd", grad_logits, near_keys, preferred_element_type=jnp.float32
            )
        )
        * inverse_root
    )
    grad_near_keys = (
        jnp.einsum(
            "sbqhk,sbqhd->sbkhd", grad_logits, query_blocks, preferred_element_type=jnp.float32
        )
        * inverse_root
    )
    grad_near_values = jnp.einsum(
        "sbqhk,sbqhd->sbkhd", fine_probs, grad_fine_numer, preferred_element_type=jnp.float32
    )
    grad_key_fine = flatten_blocks(grad_near_keys[:, :, :BLOCK]) + flatten_blocks(
        sibling_blocks(flatten_blocks(grad_near_keys[:, :, BLOCK:]))
    )
    grad_value_fine = flatten_blocks(grad_near_values[:, :, :BLOCK]) + flatten_blocks(
        sibling_blocks(flatten_blocks(grad_near_values[:, :, BLOCK:]))
    )
    cross_cots = level_cots[local_depth:]
    empty_rows = jnp.zeros((seq_count, BLOCK, width), jnp.float32)
    grad_pyramid = jnp.zeros((seq_count, 2 * BLOCK, 3, width), jnp.float32)
    for height in reversed(range(tree_depth)):
        pullback, offset, width_here, group = cross_pulls[height]
        grad_maxima, grad_totals, grad_numer = cross_cots[height]
        grad_part_query, grad_part_key, grad_part_value = pullback(
            (
                grad_maxima.reshape(seq_count, 1, width_here, HEADS),
                grad_totals.reshape(seq_count, 1, width_here, HEADS),
                grad_numer.reshape(seq_count, 1, width_here, HEADS, head_dim),
            )
        )
        query_piece = grad_part_query[:, 0]
        zero_piece = jnp.zeros_like(query_piece)
        grad_pyramid = add_at(
            grad_pyramid,
            jnp.stack([query_piece, zero_piece, zero_piece], axis=2),
            group * BLOCK + offset,
        )
        grad_pyramid = add_at(
            grad_pyramid,
            jnp.stack([empty_rows, grad_part_key[:, 0], grad_part_value[:, 0]], axis=2),
            (group ^ 1) * BLOCK,
        )
        if height > 0:
            grad_pyramid = spread_rows(grad_pyramid, 2)
    grad_block = lax.psum_scatter(grad_pyramid, "seq", scatter_dimension=1, tiled=True)
    grad_stack = grad_block
    for level_index in reversed(range(1, local_depth)):
        grad_stack = spread_rows(grad_stack, 2)
        grad_maxima, grad_totals, grad_numer = level_cots[level_index]
        grad_part_query, grad_part_key, grad_part_value = local_pulls[level_index - 1](
            (own_blocks(grad_maxima), own_blocks(grad_totals), own_blocks(grad_numer))
        )
        grad_stack = grad_stack + jnp.stack(
            [
                flatten_blocks(grad_part_query),
                flatten_blocks(sibling_blocks(flatten_blocks(grad_part_key))),
                flatten_blocks(sibling_blocks(flatten_blocks(grad_part_value))),
            ],
            axis=2,
        )
    grad_fine = spread_rows(grad_stack, 2)
    plain_shape = (seq_count, tok_count, width)
    grad_queries = (
        (grad_fine[:, :, 0] + grad_query_fine.reshape(plain_shape))
        .astype(jnp.bfloat16)
        .reshape(row_count, width)
    )
    grad_keys = (
        (grad_fine[:, :, 1] * valid_mask[..., None] + grad_key_fine.reshape(plain_shape))
        .astype(jnp.bfloat16)
        .reshape(row_count, width)
    )
    grad_values = (
        (grad_fine[:, :, 2] * valid_mask[..., None] + grad_value_fine.reshape(plain_shape))
        .astype(jnp.bfloat16)
        .reshape(row_count, width)
    )
    grad_query_weight = row_product(normed_low, grad_queries)
    grad_key_weight = row_product(normed_low, grad_keys)
    grad_value_weight = row_product(normed_low, grad_values)
    grad_query_bias = jnp.sum(grad_queries.astype(jnp.float32), axis=0)
    grad_value_bias = jnp.sum(grad_values.astype(jnp.float32), axis=0)
    grad_normed = (
        back_product(grad_queries, query_weight)
        + back_product(grad_keys, key_weight)
        + back_product(grad_values, value_weight)
    )
    grad_inputs_norm, grad_first_gain, grad_first_shift = norm_pull(
        grad_normed.reshape(plain_shape)
    )
    input_grad = grad_middle.reshape(plain_shape) + grad_inputs_norm
    summed = lax.psum(
        (
            grad_query_weight,
            grad_key_weight,
            grad_value_weight,
            grad_output_weight,
            grad_up_weight,
            grad_down_weight,
            grad_query_bias,
            grad_value_bias,
            grad_output_bias,
            grad_up_bias,
            grad_down_bias,
            grad_first_gain,
            grad_first_shift,
            grad_second_gain,
            grad_second_shift,
        ),
        ("seq", "batch"),
    )
    return (
        layer_out,
        input_grad,
        summed[0],
        summed[1],
        summed[2],
        summed[3],
        summed[4],
        summed[5],
        summed[6],
        summed[7],
        summed[8],
        summed[9],
        summed[10],
        summed[11],
        summed[12],
        summed[13],
        summed[14],
    )


def solution(mesh):
    return jax.shard_map(
        local,
        mesh=mesh,
        in_specs=(
            P("batch", "seq", None),
            P("batch"),
            P(),
            P(),
            P(),
            P(),
            P(),
            P(),
            P(),
            P(),
            P(),
            P(),
            P(),
            P(),
            P(),
            P(),
            P(),
            P("batch", "seq", None),
        ),
        out_specs=(
            P("batch", "seq", None),
            P("batch", "seq", None),
            P(),
            P(),
            P(),
            P(),
            P(),
            P(),
            P(),
            P(),
            P(),
            P(),
            P(),
            P(),
            P(),
            P(),
            P(),
        ),
        check_vma=False,
    )
```

profile of v0, /device:TPU:0, one launch (start us, length us, event | category | flops | bytes accessed | tf_op | source)
XLA Modules:
  0.0 1029.2 jit_solution(11046199558042101359)
XLA Ops:
  30.9 29.1 %maximum_reduce_fusion = f32[4,128,3,512]{3,1,0,2:T(8,128)} fusion(f32[4,128,2,1,512]{4,2,1,0,3:T(2,128)S(1)} %get-tuple-element.100, f32[4,128,2,1,512]{4,2,1,0,3:T(2,128)S(1)} %get-tuple-element.99, f32[4,128,2,1,512]{4,2,1,0,3:T(2,128)S(1)} %copy-done.71), kind=kLoop, calls=%fused_computation.12 | loop fusion | flops 3932160 | bytes 9437184 | tf_op jit(solution)/shard_map/reduce_sum | solution.py:68
  60.0 5.4 reshape.1826
  65.4 6.8 reduce_sum.653
  86.6 9.5 all-gather
  268.9 5.5 fusion.59
  278.1 4.8 reshape.1844
  291.9 5.2 reshape.1846
  306.1 4.8 reshape.1848
  333.1 4.8 reshape_broadcast_in_dim_reshape.22
  378.0 4.8 reshape.1850
  388.0 4.8 reshape.1852
  411.6 12.9 %divide_convert_fusion = bf16[1024,512]{0,1:T(8,128)(2,1)} fusion(f32[1024,512]{0,1:T(8,128)} %bitcast.980, f32[1024,512]{0,1:T(8,128)} %bitcast.974, f32[1024,512]{0,1:T(8,128)} %copy.2337, f32[1024,512]{0,1:T(8,128)} %bitcast.975, f32[1024,512]{0,1:T(8,128)} %copy.2333, f32[1024,512]{0,1:T(8,128)} %bitcast.976, f32[1024,512]{0,1:T(8,128)} %copy.2328, ...), kind=kLoop, calls=%fused_computation.90 | loop fusion | flops 6815744 | bytes 28311552 | tf_op jit(solution)/shard_map/convert_element_type | solution.py:255
  427.5 5.9 multiply_convert_fusion
  433.5 9.0 convert_reduce_fusion
  476.2 7.3 multiply_reduce_fusion.8
  514.1 4.7 multiply_reduce_fusion.4
  539.3 4.9 multiply_reduce_fusion.1
  558.1 5.9 multiply_reduce_fusion
  569.4 4.7 fusion.28
  578.5 5.7 multiply_bitcast_fusion.2
  586.4 9.0 convolution_bitcast_fusion
  595.5 6.0 fusion.8
  624.1 6.3 copy.2560
  634.4 5.0 rev.73
  662.3 4.8 reshape_reshape.49
  667.0 4.8 mul.1043
  671.8 6.2 copy.2564
  678.0 5.1 reshape.1923
  692.8 4.6 rev.72
  697.5 4.8 reshape_reshape.48
  702.3 6.1 copy.2562
  708.4 5.3 reshape.1922
  715.5 6.8 fusion.212
  722.3 4.7 fusion.199
  740.7 5.4 reshape.1912
  749.4 4.5 broadcast_in_dim.622
  753.9 8.8 reshape.1918
  774.5 4.8 reshape_reshape.50
  779.3 5.0 reshape_reshape.47
  784.3 4.8 mul.1047
  789.1 4.9 mul.1029
  794.0 4.8 reshape.1924
  798.9 4.8 reshape.1920
  803.6 4.9 reshape_reshape.45
  808.5 5.1 reshape.1919
  813.7 6.7 add_convert_fusion.2
  833.5 41.4 %all-reduce.2 = (f32[512]{0:T(512)}, f32[512]{0:T(512)}, f32[512]{0:T(512)}, f32[2048]{0:T(1024)}, f32[512]{0:T(512)}, /*index=5*/f32[512]{0:T(512)}, f32[512]{0:T(512)}, f32[512]{0:T(512)}, f32[512]{0:T(512)}) all-reduce(f32[512]{0:T(512)S(1)} %get-tuple-element.18, ...), channel_id=1, replica_groups=mesh['seq'=4,'batch'=8] {'seq','batch'}, use_global_device_ids=true, to_apply=%region_70.71 | all-reduce | flops 6144 | bytes 49152 | tf_op jit(solution)/shard_map/psum | solution.py:388
  877.9 132.2 %all-reduce.6.cloned.1.call-done = (f32[512,512]{1,0:T(8,128)}, f32[512,512]{1,0:T(8,128)}, f32[512,512]{1,0:T(8,128)}, f32[512,512]{1,0:T(8,128)}, f32[512,2048]{1,0:T(8,128)}, /*index=5*/f32[2048,512]{1,0:T(8,128)}) async-done(((f32[512,512]{1,0:T(8,128)}, f32[512,512]{1,0:T(8,128)}, f32[512,512]{1,0:T(8,128)}, f32[512,512]{1,0:T(8,128)}, f32[512,2048]{1,0:T(8,128)}, /*index=5*/f32[2048,512]{1,0:T(8,128)}), ...) | async-done | bytes 12582928 | tf_op jit(solution)/shard_map/psum | solution.py:388
  (1121 shorter events, 547.0 us)
Async XLA Ops:
  7.2 420.0 %copy-start = (bf16[512,2048]{1,0:T(8,128)(2,1)S(1)}, bf16[512,2048]{1,0:T(8,128)(2,1)}, u32[]{:S(2)}) copy-start(bf16[512,2048]{1,0:T(8,128)(2,1)} %param.24) | copy-start | bytes 6291460
  7.2 339.2 %all-gather.3.cloned.1.call-start = ((), (), s32[]{:S(2)}) async-start(), calls=%async_computation.1 | async-start | bytes 1966080 | tf_op jit(solution)/shard_map/all_gather | solution.py:222
  82.6 19.2 %copy-start.35 = (bf16[1024,512]{1,0:T(8,128)(2,1)S(1)}, bf16[1024,512]{1,0:T(8,128)(2,1)}, u32[]{:S(2)}) copy-start(bf16[1024,512]{1,0:T(8,128)(2,1)} %convolution_convert_fusion.1) | copy-start | bytes 3145732
  82.7 644.3 %reduce-scatter.2.cloned.1.call-start = ((), (), s32[]{:S(2)}) async-start(), calls=%async_computation.2 | async-start | bytes 1966080 | tf_op jit(solution)/shard_map/reduce_scatter | solution.py:341
  123.0 78.3 %copy-start.14 = (f32[4,2,8,16,16]{4,3,2,1,0:T(8,128)}, f32[4,2,8,16,16]{4,3,2,1,0:T(8,128)S(1)}, u32[]{:S(2)}) copy-start(f32[4,2,8,16,16]{4,3,2,1,0:T(8,128)S(1)} %get-tuple-element.130) | copy-start | bytes 196612
  123.0 78.3 %copy-start.115 = (f32[4,2,16,8]{2,3,1,0:T(8,128)}, f32[4,2,16,8]{2,3,1,0:T(8,128)S(1)}, u32[]{:S(2)}) copy-start(f32[4,2,16,8]{2,3,1,0:T(8,128)S(1)} %get-tuple-element.129) | copy-start | bytes 12292
  136.8 188.0 %copy-start.185 = (f32[4,16,32]{2,1,0:T(8,128)}, f32[4,16,32]{2,1,0:T(8,128)S(1)}, u32[]{:S(2)}) copy-start(f32[4,16,32]{2,1,0:T(8,128)S(1)} %pad_maximum_fusion.12) | copy-start | bytes 24580
  141.6 183.2 %copy-start.37 = (f32[4,16,16,8]{2,3,1,0:T(8,128)}, f32[4,16,16,8]{2,3,1,0:T(8,128)S(1)}, u32[]{:S(2)}) copy-start(f32[4,16,16,8]{2,3,1,0:T(8,128)S(1)} %get-tuple-element.135) | copy-start | bytes 98308
  144.3 9.6 copy-start.89
  186.2 15.2 %copy-start.74 = (f32[4,2,16,8,64]{4,3,2,1,0:T(8,128)S(1)}, f32[4,2,16,8,64]{4,3,2,1,0:T(8,128)}, u32[]{:S(2)}) copy-start(f32[4,2,16,8,64]{4,3,2,1,0:T(8,128)} %get-tuple-element.115) | copy-start | bytes 786436
  211.2 31.1 %copy-start.5 = (f32[4,4,8,16,16]{4,3,2,1,0:T(8,128)}, f32[4,4,8,16,16]{4,3,2,1,0:T(8,128)S(1)}, u32[]{:S(2)}) copy-start(f32[4,4,8,16,16]{4,3,2,1,0:T(8,128)S(1)} %get-tuple-element.132) | copy-start | bytes 393220
  211.2 31.1 %copy-start.84 = (f32[4,4,16,8]{2,3,1,0:T(8,128)}, f32[4,4,16,8]{2,3,1,0:T(8,128)S(1)}, u32[]{:S(2)}) copy-start(f32[4,4,16,8]{2,3,1,0:T(8,128)S(1)} %get-tuple-element.131) | copy-start | bytes 24580
  214.4 16.5 %copy-start.222 = (f32[4,64,8]{1,2,0:T(8,128)}, f32[4,64,8]{1,2,0:T(8,128)S(1)}, u32[]{:S(2)}) copy-start(f32[4,64,8]{1,2,0:T(8,128)S(1)} %broadcast_in_dim.504) | copy-start | bytes 24580
  215.4 17.5 %copy-start.224 = (f32[4,64,8]{1,2,0:T(8,128)}, f32[4,64,8]{1,2,0:T(8,128)S(1)}, u32[]{:S(2)}) copy-start(f32[4,64,8]{1,2,0:T(8,128)S(1)} %broadcast_in_dim.484) | copy-start | bytes 24580
  257.5 11.5 %copy-start.46 = (f32[4,8,16,8]{2,3,1,0:T(8,128)}, f32[4,8,16,8]{2,3,1,0:T(8,128)S(1)}, u32[]{:S(2)}) copy-start(f32[4,8,16,8]{2,3,1,0:T(8,128)S(1)} %get-tuple-element.133) | copy-start | bytes 49156
  356.4 17.9 %copy-start.105 = (f32[4,16,8,64]{3,2,1,0:T(8,128)}, f32[4,16,8,64]{3,2,1,0:T(8,128)S(1)}, u32[]{:S(2)}) copy-start(f32[4,16,8,64]{3,2,1,0:T(8,128)S(1)} %get-tuple-element.121) | copy-start | bytes 393220
  356.4 8.0 copy-start.174
  364.4 9.9 copy-start.180
  368.6 9.4 copy-start.123
  411.6 12.9 %copy-start.8 = (bf16[4,256,512]{2,1,0:T(8,128)(2,1)S(1)}, bf16[4,256,512]{2,1,0:T(8,128)(2,1)}, u32[]{:S(2)}) copy-start(bf16[4,256,512]{2,1,0:T(8,128)(2,1)} %param.18) | copy-start | bytes 3145732
  426.7 19.1 %copy-start.12 = (f32[1024,512]{1,0:T(8,128)}, f32[1024,512]{1,0:T(8,128)S(1)}, u32[]{:S(2)}) copy-start(f32[1024,512]{1,0:T(8,128)S(1)} %get-tuple-element.138) | copy-start | bytes 6291460
  426.8 19.1 %copy-start.220 = (f32[1024]{0:T(1024)}, f32[1024]{0:T(1024)S(1)}, u32[]{:S(2)}) copy-start(f32[1024]{0:T(1024)S(1)} %broadcast_multiply_fusion.2) | copy-start | bytes 12292
  427.5 18.3 %copy-start.234 = (f32[1024]{0:T(1024)}, f32[1024]{0:T(1024)S(1)}, u32[]{:S(2)}) copy-start(f32[1024]{0:T(1024)S(1)} %fusion.175) | copy-start | bytes 12292
  476.2 8.4 copy-start.227
  476.2 9.1 copy-start.226
  483.6 9.2 copy-start.147
  484.7 10.9 %copy-start.38 = (f32[4,16,16,8]{2,3,1,0:T(8,128)S(1)}, f32[4,16,16,8]{2,3,1,0:T(8,128)}, u32[]{:S(2)}) copy-start(f32[4,16,16,8]{2,3,1,0:T(8,128)} %copy-done.37) | copy-start | bytes 98308
  484.7 10.9 %copy-start.102 = (f32[4,16,16,8]{2,1,3,0:T(8,128)S(1)}, f32[4,16,16,8]{2,1,3,0:T(8,128)}, u32[]{:S(2)}) copy-start(f32[4,16,16,8]{2,1,3,0:T(8,128)} %reshape.1886) | copy-start | bytes 98308
  484.7 10.9 %copy-start.103 = (f32[4,16,16,8]{2,3,1,0:T(8,128)S(1)}, f32[4,16,16,8]{2,3,1,0:T(8,128)}, u32[]{:S(2)}) copy-start(f32[4,16,16,8]{2,3,1,0:T(8,128)} %copy.2429) | copy-start | bytes 98308
  484.7 10.9 %copy-start.104 = (f32[4,16,16,8]{2,3,1,0:T(8,128)S(1)}, f32[4,16,16,8]{2,3,1,0:T(8,128)}, u32[]{:S(2)}) copy-start(f32[4,16,16,8]{2,3,1,0:T(8,128)} %copy.2427) | copy-start | bytes 98308
  518.8 7.8 copy-start.165
  518.8 7.8 copy-start.166
  518.9 7.8 copy-start.167
  518.9 7.8 copy-start.168
  518.9 7.8 copy-start.171
  518.9 7.8 copy-start.172
  518.9 7.8 copy-start.206
  518.9 7.8 copy-start.208
  518.9 7.8 copy-start.255
  586.3 9.1 copy-start.27
  586.3 9.1 copy-start.29
  586.3 9.1 copy-start.56
  586.3 9.1 copy-start.57
  586.3 9.1 copy-start.136
  586.4 9.1 copy-start.209
  586.4 9.1 copy-start.211
  622.4 387.7 %all-reduce.6.cloned.1.call-start = ((), (), s32[]{:S(2)}) async-start(), calls=%async_computation.3 | async-start | bytes 25165824 | tf_op jit(solution)/shard_map/psum | solution.py:388
  753.9 8.8 copy-start.18
  (273 other events, 992.5 us)
Sparse Core Ops, SparseCore 0:
  82.8 33.6 all-gather.2
  622.5 31.2 reduce-scatter.1
  773.2 236.8 all-reduce.5
where the time goes:
time: 1040 us; the launch traced here: 1030 us
  local copies, waits for them, and re-layouts  515 us (50%)
  other arithmetic  157 us (15%)
  matrix products  155 us (15%)
  waiting for transfers between devices  132 us (13%)
  blocking collectives  50.9 us (5%)
  between operations  18.4 us (2%)
    psum x1, waiting for transfers between devices, local(): lax.psum((grad_query_weight, grad_key_weight, grad_value_weight, grad_out...  132 us
    reshape x50, local copies, waits for them, and re-layouts, spread_rows(): return widened.reshape((leading[0], leading[1] * factor) + array.shape[2:])  113 us
    reduce_sum x23, other arithmetic, collapse_rows(): jnp.sum(array.reshape((array.shape[0], array.shape[1] // factor, factor)...  70.4 us
    broadcast_in_dim x82, local copies, waits for them, and re-layouts, spread_rows(): jnp.broadcast_to(array[:, :, None], leading + (factor,) + array.shape[2:])  60.9 us
    unnamed x669, local copies, waits for them, and re-layouts  50.6 us
    psum x1, blocking collectives, local(): lax.psum((grad_query_weight, grad_key_weight, grad_value_weight, grad_out...  41.4 us
    dot_general x15, matrix products, coarse_attend(): jnp.einsum('sbqhd,sbkhd->sbqhk', query_means, key_means, precision=HIGHEST)  35.8 us
    rev x17, local copies, waits for them, and re-layouts, sibling_blocks(): paired[:, :, ::-1]  35.7 us
  transfers between devices with their start and end apart: 3, of which 1 were waited for; matrix products, arithmetic and copies ran while one was open for 40% of the time, Pallas kernels for 0%

commit v1 on v0

v1 whole, which is shorter than its diff:
```python
import functools

import jax
import jax.numpy as jnp
import numpy as np
from jax import lax
from jax.experimental import pallas as pl
from jax.experimental.pallas import tpu as pltpu
from jax.sharding import PartitionSpec as P

HEADS = 8
BLOCK = 16
CHUNK = 128
PAIR = 128
HALF = 64
LOCAL_ROWS = (128, 64, 32, 16)
LOCAL_STARTS = (0, 128, 192, 224)
LOCAL_KEYS = 240
COARSE_KEYS = 112
MASKED = -1e30
TOKEN = (8, 128)
ROUND_BYTES = dict(down=40_000_000, up=40_000_000, last=40_000_000)
ROUNDS = "u,d,ud,dudldluudlldulduluoludluldlul"
TILE = 32
EPSILON = 1e-05
VMEM_BYTES = 62 * 2**20
F32 = jnp.float32
BF16 = jnp.bfloat16


def dot(left, right):
    return lax.dot_general(left, right, (((1,), (0,)), ((), ())), preferred_element_type=F32)


def dot_nt(left, right):
    return lax.dot_general(left, right, (((1,), (1,)), ((), ())), preferred_element_type=F32)


def dot_tn(left, right):
    return lax.dot_general(left, right, (((0,), (0,)), ((), ())), preferred_element_type=F32)


def iota(shape, axis):
    return lax.broadcasted_iota(jnp.int32, shape, axis)


def row_mean(values):
    return jnp.mean(values, axis=-1, keepdims=True)


def column_sum(values):
    return jnp.sum(values, axis=0, keepdims=True)


def normalize(values):
    center = values - row_mean(values)
    scale = lax.rsqrt(row_mean(center * center) + EPSILON)
    return center * scale, scale


def normalize_back(grads, normed, scale):
    return scale * (grads - row_mean(grads) - normed * row_mean(grads * normed))


def block_diagonal(block):
    zeros = jnp.zeros((HALF, CHUNK), block.dtype)
    first = jnp.concatenate([block[:HALF], zeros], axis=1)
    second = jnp.concatenate([zeros, block[HALF:]], axis=1)
    return jnp.concatenate([first, second], axis=0)


def diagonal_blocks(wide):
    return jnp.concatenate([wide[:HALF, :CHUNK], wide[HALF:, CHUNK:]], axis=0)


def head_rows(row):
    first = jnp.broadcast_to(row[:, :CHUNK], (HALF, CHUNK))
    second = jnp.broadcast_to(row[:, CHUNK:], (HALF, CHUNK))
    return jnp.concatenate([first, second], axis=0)


def twice(block):
    return jnp.concatenate([block, block], axis=1)


def four_times(block):
    return jnp.concatenate([block, block, block, block], axis=1)


def averaging(level):
    spots = np.arange(CHUNK) >> level
    return (spots[:, None] == spots[None, :]).astype(np.float32) / (1 << level)


def averaging_pair(level):
    return np.kron(np.eye(2, dtype=np.float32), averaging(level))


def coarse_members(tok_count):
    spots = np.arange(tok_count)
    rows = []
    for chunk in range(2):
        for level in range(1, 4):
            first = (chunk if level < 3 else 1 - chunk) * CHUNK
            begins = first + (np.arange(LOCAL_ROWS[level]) << level)
            inside = spots[None, :] - begins[:, None]
            rows.append((inside >= 0) & (inside < (1 << level)))
    return np.concatenate(rows, axis=0).astype(np.float32)


def group_members(tok_count, factor):
    spots = np.arange(tok_count) // factor
    return (np.arange(tok_count // factor)[:, None] == spots[None, :]).astype(np.float32)


def local_counts(remaining, chunk, level):
    rows = LOCAL_ROWS[level]
    spots = iota((rows, CHUNK), 0) << level
    first = (chunk if level < 3 else 1 - chunk) * CHUNK
    return jnp.clip(remaining - (first + spots), 0, 1 << level), spots


def local_bias(remaining, chunk):
    parts = []
    for level in range(4):
        counts, spots = local_counts(remaining, chunk, level)
        allowed = counts > 0
        places = iota(counts.shape, 1)
        if level == 0:
            allowed = allowed & ((spots >> 5) == (places >> 5))
        elif level < 3:
            allowed = allowed & (((spots >> (4 + level)) ^ (places >> (4 + level))) == 1)
        logs = jnp.log(jnp.maximum(counts, 1).astype(F32))
        parts.append(jnp.where(allowed, logs, MASKED))
    return parts


def coarse_inverse(remaining):
    parts = []
    for chunk in range(2):
        for level in range(1, 4):
            counts, _ = local_counts(remaining, chunk, level)
            parts.append(1.0 / jnp.maximum(counts, 1).astype(F32))
    return jnp.concatenate(parts, axis=0)


def pooled_keys(members, rows, inverse):
    return (dot(members, rows) * four_times(inverse)).astype(BF16)


def chunk_keys(rows, pooled):
    return [
        jnp.concatenate(
            [
                rows[chunk * CHUNK : (chunk + 1) * CHUNK],
                pooled[chunk * COARSE_KEYS : (chunk + 1) * COARSE_KEYS],
            ],
            axis=0,
        )
        for chunk in range(2)
    ]


def level_queries(queries, coarse, chunk):
    levels = coarse.shape[1] // CHUNK // 2
    parts = [queries[:, chunk * CHUNK : (chunk + 1) * CHUNK]]
    for at in range(chunk * levels, (chunk + 1) * levels):
        parts.append(coarse[:, at * CHUNK : (at + 1) * CHUNK])
    return parts


UNITS = [(chunk, pair) for chunk in range(2) for pair in range(HEADS // 2)]


def skewed(first, *stages):
    held = {}
    for tick in range(len(UNITS) + len(stages)):
        for stage in range(len(stages) + 1):
            at = tick - stage
            if 0 <= at < len(UNITS):
                unit = UNITS[at]
                if stage == 0:
                    held[unit] = first(unit)
                else:
                    held[unit] = stages[stage - 1](unit, held[unit])
    return held


def interleaved(work, count):
    runs = [work(at) for at in range(count)]
    while runs:
        runs = [run for run in runs if next(run, run) is not run]


def pair_of(index):
    return slice(index * PAIR, (index + 1) * PAIR)


def local_logits(keys, tall, pair):
    return [
        dot(
            keys[LOCAL_STARTS[level] : LOCAL_STARTS[level] + LOCAL_ROWS[level], pair_of(pair)],
            tall[level],
        )
        for level in range(4)
    ]


def tiles(rows, size=TILE):
    return [slice(begin, begin + size) for begin in range(0, rows, size)]


def partial_sum(values):
    return jnp.sum(values.reshape(-1, 8, values.shape[1]), axis=0)


def add_to(ref, values):
    for rows in tiles(values.shape[0]):
        ref[rows, :] += values[rows]


def project_kernel(
    heights,
    lengths_ref,
    shard_ref,
    tokens_ref,
    query_weight_ref,
    key_weight_ref,
    value_weight_ref,
    query_bias_ref,
    value_bias_ref,
    gain_ref,
    shift_ref,
    groups_ref,
    queries_ref,
    keys_ref,
    values_ref,
    *refs,
):
    sums_refs, normed_ref, turned_ref = refs[:heights], refs[heights], refs[heights + 1]
    count, tok_count, width = tokens_ref.shape
    gain, shift = gain_ref[...], shift_ref[...]
    for at in range(count):
        for rows in tiles(tok_count):
            normed, _ = normalize(tokens_ref[at, rows].astype(F32))
            normed_ref[at, rows] = (normed * gain + shift).astype(BF16)
    normed = normed_ref[...].reshape(count * tok_count, width)
    keys_wide = dot(normed, key_weight_ref[...])
    values_wide = dot(normed, value_weight_ref[...])
    queries_wide = dot(normed, query_weight_ref[...])
    value_bias, query_bias = value_bias_ref[...], query_bias_ref[...]
    for at in range(count):
        remaining = lengths_ref[pl.program_id(0) * count + at] - shard_ref[0] * tok_count
        for rows in tiles(tok_count):
            places = slice(at * tok_count + rows.start, at * tok_count + rows.stop)
            valid = iota((TILE, width), 0) + rows.start < remaining
            keys_ref[at, rows] = jnp.where(valid, keys_wide[places], 0.0).astype(BF16)
            values = values_wide[places] + value_bias
            values_ref[at, rows] = jnp.where(valid, values, 0.0).astype(BF16)
            turned_ref[at, rows] = ((queries_wide[places] + query_bias) * 0.125).astype(BF16)
        key_sums = dot(groups_ref[...], keys_ref[at])
        value_sums = dot(groups_ref[...], values_ref[at])
        begin = 0
        for height in range(heights):
            size = BLOCK >> height
            sums_refs[height][at, :, :width] = key_sums[begin : begin + size]
            sums_refs[height][at, :, width:] = value_sums[begin : begin + size]
            begin += max(size, 8)
        queries_ref[at] = turned_ref[at].T


def near_kernel(
    lengths_ref,
    shard_ref,
    queries_ref,
    keys_ref,
    values_ref,
    members_ref,
    spread_ref,
    maxima_ref,
    totals_ref,
    numer_ref,
    coarse_ref,
    pooled_keys_ref,
    pooled_values_ref,
):
    sequence = pl.program_id(0)
    tok_count = keys_ref.shape[1]
    remaining = lengths_ref[sequence] - shard_ref[0] * tok_count
    inverse = coarse_inverse(remaining)
    pooled_keys_ref[0] = pooled_keys(members_ref[...], keys_ref[0], inverse)
    pooled_values_ref[0] = pooled_keys(members_ref[...], values_ref[0], inverse)
    keys = chunk_keys(keys_ref[0], pooled_keys_ref[0])
    values = chunk_keys(values_ref[0], pooled_values_ref[0])
    queries = queries_ref[0]
    bias = [local_bias(remaining, chunk) for chunk in range(2)]
    columns = spread_ref.shape[1]
    for chunk in range(2):
        own = queries[:, chunk * CHUNK : (chunk + 1) * CHUNK]
        coarse_ref[0, :, chunk * columns : (chunk + 1) * columns] = dot(
            own, spread_ref[...]
        ).astype(BF16)
    coarse = coarse_ref[0]
    levels = [level_queries(queries, coarse, chunk) for chunk in range(2)]

    def logits_of(unit):
        chunk, pair = unit
        tall = [block_diagonal(part[pair_of(pair)]) for part in levels[chunk]]
        return local_logits(keys[chunk], tall, pair)

    def softmax_of(unit, logits):
        chunk, pair = unit
        lanes = slice(chunk * CHUNK, (chunk + 1) * CHUNK)
        both = []
        for side in range(2):
            half = slice(side * CHUNK, (side + 1) * CHUNK)
            head = 2 * pair + side
            parts = [part[:, half] + extra for part, extra in zip(logits, bias[chunk])]
            maxima = functools.reduce(
                jnp.maximum, [jnp.max(part, axis=0, keepdims=True) for part in parts]
            )
            parts = [jnp.exp(part - maxima) for part in parts]
            maxima_ref[0, head : head + 1, lanes] = maxima
            totals = sum(partial_sum(part) for part in parts)
            totals_ref[0, head : head + 1, lanes] = column_sum(totals)
            both.append(jnp.concatenate([part.astype(BF16) for part in parts], axis=0))
        return jnp.concatenate(both, axis=1)

    def numer_of(unit, powers):
        chunk, pair = unit
        lanes = slice(chunk * CHUNK, (chunk + 1) * CHUNK)
        wide = dot_tn(values[chunk][:, pair_of(pair)], powers)
        numer_ref[0, pair_of(pair), lanes] = diagonal_blocks(wide).astype(BF16)

    skewed(logits_of, softmax_of, numer_of)


def split_rows(source_ref, core, send_ref, keep_ref):
    rows = send_ref.shape[0]
    send_ref[...] = source_ref[pl.ds(pl.multiple_of((1 - core) * rows, 8), rows), :]
    keep_ref[...] = source_ref[pl.ds(pl.multiple_of(core * rows, 8), rows), :]


def far_counts(length, shard, tok_count, heights, shards):
    spots = iota((BLOCK * heights, CHUNK), 0)
    begins = jnp.zeros_like(spots)
    widths = jnp.ones_like(spots)
    row = 0
    for mask in range(1, shards):
        height = mask.bit_length() - 1
        rows = BLOCK >> height
        inside = (spots >= row) & (spots < row + rows)
        first = jnp.bitwise_xor(shard, mask) * tok_count
        begins = jnp.where(inside, first + ((spots - row) << (4 + height)), begins)
        widths = jnp.where(inside, BLOCK << height, widths)
        row += rows
    return jnp.minimum(jnp.maximum(length - begins, 0), widths)


def half_lanes(shape, side):
    return iota(shape, 1) // HALF == side


def by_head(rows):
    blocks = []
    for head in range(HEADS):
        parts = [jnp.zeros((BLOCK, PAIR), F32)] * (HEADS // 2)
        part = rows[:, pair_of(head // 2)]
        parts[head // 2] = jnp.where(half_lanes(part.shape, head % 2), part, 0.0)
        blocks.append(jnp.concatenate(parts, axis=1))
    return jnp.concatenate(blocks, axis=0).astype(BF16)


def of_heads(wide):
    parts = []
    for pair in range(HEADS // 2):
        first = wide[2 * pair * BLOCK : (2 * pair + 1) * BLOCK, pair_of(pair)]
        second = wide[(2 * pair + 1) * BLOCK : (2 * pair + 2) * BLOCK, pair_of(pair)]
        parts.append(jnp.where(half_lanes(first.shape, 0), first, second))
    return jnp.concatenate(parts, axis=1)


def far_state(sequence, lengths_ref, shard, tok_count, heights, shards, pieces):
    counts = far_counts(lengths_ref[sequence], shard, tok_count, heights, shards)
    floored = jnp.maximum(counts, 1).astype(F32)
    inverse = four_times(1.0 / floored)
    bias = twice(jnp.where(counts > 0, jnp.log(floored), MASKED))
    bias = [bias[BLOCK * at : BLOCK * (at + 1)] for at in range(heights)]
    sums = jnp.concatenate([piece[sequence] for piece in pieces], axis=0)
    width = sums.shape[1] // 2
    keys, values = [], []
    for at in range(heights):
        rows = slice(BLOCK * at, BLOCK * (at + 1))
        keys.append(by_head(sums[rows, :width] * inverse[rows]))
        values.append(by_head(sums[rows, width:] * inverse[rows]))
    return keys, jnp.concatenate(values, axis=0), bias, inverse


def far_queries_of(queries, spread_ref, heights):
    return [dot(queries, spread_ref[at]).astype(BF16) for at in range(heights)]


def join_kernel(
    heights,
    shards,
    piece_count,
    lengths_ref,
    shard_ref,
    tokens_ref,
    queries_ref,
    maxima_ref,
    totals_ref,
    numer_ref,
    output_weight_ref,
    output_bias_ref,
    gain_ref,
    shift_ref,
    spread_ref,
    *refs,
):
    pieces = refs[:piece_count]
    middle_ref, second_ref, outs_ref, level_ref, far_ref, attended_ref = refs[piece_count:]
    count, tok_count, _ = tokens_ref.shape
    bias, gain, shift = output_bias_ref[...], gain_ref[...], shift_ref[...]

    def work(own):
        far_keys, far_values, far_bias, _ = far_state(
            pl.program_id(0) * count + own, lengths_ref, shard_ref[0], tok_count, heights, shards, pieces
        )
        coarse = far_queries_of(queries_ref[own], spread_ref, heights)
        for at in range(heights):
            far_ref[own, :, at * tok_count : (at + 1) * tok_count] = coarse[at]
        logits = [dot(far_keys[at], coarse[at]) for at in range(heights)]
        yield
        powers = [[] for _ in range(heights)]
        fades, inverses = [], []
        for head in range(HEADS):
            rows = slice(BLOCK * head, BLOCK * (head + 1))
            near_maxima = maxima_ref[own, head : head + 1, :]
            parts = [logits[at][rows] + far_bias[at] for at in range(heights)]
            maxima = functools.reduce(jnp.maximum, parts)
            maxima = jnp.maximum(near_maxima, jnp.max(maxima, axis=0, keepdims=True))
            fade = jnp.exp(near_maxima - maxima)
            parts = [jnp.exp(part - maxima) for part in parts]
            totals = fade * totals_ref[own, head : head + 1, :] + column_sum(sum(parts))
            for at in range(heights):
                powers[at].append(parts[at].astype(BF16))
            level_ref[own, head : head + 1, :] = maxima + jnp.log(totals)
            inverse = 1.0 / totals
            fades.append(fade * inverse)
            inverses.append(inverse)
        yield
        far_numer = dot_tn(far_values, jnp.concatenate(sum(powers, []), axis=0))
        yield
        for head in range(HEADS):
            rows = slice(HALF * head, HALF * (head + 1))
            outs = numer_ref[own, rows, :].astype(F32) * fades[head] + far_numer[rows] * inverses[head]
            outs_ref[own, rows, :] = outs
            attended_ref[own, rows, :] = outs.astype(BF16)
        yield
        projected = dot_tn(attended_ref[own], output_weight_ref[...])
        yield
        for rows in tiles(tok_count):
            middle = tokens_ref[own, rows].astype(F32) + projected[rows] + bias
            middle_ref[own, rows] = middle
            normed, _ = normalize(middle)
            second_ref[own, rows] = (normed * gain + shift).astype(BF16)

    interleaved(work, count)


def hidden_kernel(
    step_count,
    core_ref,
    second_ref,
    cotangent_ref,
    up_weight_ref,
    down_weight_ref,
    up_bias_ref,
    grad_second_ref,
    down_send_ref,
    down_keep_ref,
    up_send_ref,
    up_keep_ref,
    bias_ref,
    hidden_ref,
    total_ref,
    second_turned_ref,
    grad_hidden_ref,
):
    step = pl.program_id(0)
    seq_count, tok_count, width = second_ref.shape

    @pl.when(step == 0)
    def _():
        total_ref[...] = jnp.zeros_like(total_ref)
        for at in range(seq_count):
            second_turned_ref[:, at * tok_count : (at + 1) * tok_count] = second_ref[at].T

    up_weight, down_weight = up_weight_ref[...], down_weight_ref[...]

    together = 2 - seq_count % 2
    block = together * tok_count

    def flat(ref, at):
        return ref[at * together : (at + 1) * together].reshape(block, width)

    def products(at):
        return (
            dot(flat(second_ref, at), up_weight),
            dot_nt(flat(cotangent_ref, at), down_weight),
        )

    up_bias = up_bias_ref[...]

    def bend(at, state):
        bias = 0.0
        for rows in tiles(block, TILE // 2):
            hidden_in = state[0][rows] + up_bias
            squares = hidden_in * hidden_in
            bent = jnp.tanh(hidden_in * (0.7978845608028654 + 0.035677408136300125 * squares))
            rising = 0.5 + 0.5 * bent
            slope = rising + hidden_in * (0.5 - 0.5 * bent * bent) * (
                0.7978845608028654 + 0.10703222440890037 * squares
            )
            grad_hidden = (state[1][rows] * slope).astype(BF16)
            places = slice(at * block + rows.start, at * block + rows.stop)
            hidden_ref[places, :] = (hidden_in * rising).astype(BF16)
            grad_hidden_ref[places, :] = grad_hidden
            bias = bias + partial_sum(grad_hidden.astype(F32))
        return bias

    def spread(at):
        rows = slice(at * block, (at + 1) * block)
        grads = dot_nt(grad_hidden_ref[rows, :], up_weight)
        for rows in tiles(block):
            sequence = at * together + rows.start // tok_count
            begin = rows.start % tok_count
            places = slice(begin, begin + TILE)
            total_ref[sequence, places] += grads[rows]

    state = products(0)
    bias = 0.0
    for at in range(seq_count // together):
        later = products(at + 1) if at + 1 < seq_count // together else None
        bias = bias + bend(at, state)
        spread(at)
        state = later
    bias_ref[...] = column_sum(bias)
    down = dot_tn(hidden_ref[...], cotangent_ref[...].reshape(seq_count * tok_count, width))
    up = dot(second_turned_ref[...], grad_hidden_ref[...]).reshape(up_send_ref.shape)

    @pl.when(step < step_count // 2)
    def _():
        down_send_ref[0] = down
        up_send_ref[...] = up

    @pl.when(step >= step_count // 2)
    def _():
        down_keep_ref[0] = down
        up_keep_ref[...] = up

    @pl.when(step == step_count - 1)
    def _():
        for at in range(seq_count):
            for rows in tiles(tok_count):
                grad_second_ref[at, rows] = total_ref[at, rows].astype(BF16)


def output_kernel(
    core_ref, hidden_ref, middle_ref, down_weight_ref, down_bias_ref, layer_ref
):
    results = dot(hidden_ref[...], down_weight_ref[...])
    bias = down_bias_ref[...]
    for rows in tiles(results.shape[0]):
        layer_ref[0, rows] = (middle_ref[0, rows] + results[rows] + bias).astype(BF16)


def backward_kernel(
    heights,
    shards,
    piece_count,
    lengths_ref,
    shard_ref,
    cotangent_ref,
    far_ref,
    middle_ref,
    outs_ref,
    level_ref,
    grad_second_ref,
    output_weight_ref,
    gain_ref,
    spread_ref,
    *refs,
):
    pieces = refs[:piece_count]
    refs = refs[piece_count + 2 :]
    grad_middle_ref, grad_attended_ref, inner_ref, grad_queries_ref = refs[:4]
    grad_pieces = refs[4 : piece_count + 4]
    send_ref, keep_ref, small_ref, weights_ref, project_ref, attended_ref = refs[piece_count + 4 :]
    step = pl.program_id(0)
    count, tok_count, width = middle_ref.shape

    @pl.when(step == 0)
    def _():
        weights_ref[...] = jnp.zeros_like(weights_ref)
        small_ref[...] = jnp.zeros_like(small_ref)

    gain = gain_ref[...]

    def work(own):
        far_keys, far_values, far_bias, inverse = far_state(
            step * count + own, lengths_ref, shard_ref[0], tok_count, heights, shards, pieces
        )
        coarse = [far_ref[own, :, at * tok_count : (at + 1) * tok_count] for at in range(heights)]
        logits = [dot(far_keys[at], coarse[at]) for at in range(heights)]
        yield
        small = [0.0] * 4
        for rows in tiles(tok_count):
            normed, scale = normalize(middle_ref[own, rows])
            grad_second = grad_second_ref[own, rows].astype(F32)
            grad_result = cotangent_ref[own, rows].astype(F32)
            grad_middle = grad_result + normalize_back(grad_second * gain, normed, scale)
            grad_middle_ref[own, rows] = grad_middle
            grad_project = grad_middle.astype(BF16)
            project_ref[own, rows] = grad_project
            sums = [grad_result, grad_second * normed, grad_second, grad_project.astype(F32)]
            small = [total + partial_sum(part) for total, part in zip(small, sums)]
        for at, total in enumerate(small):
            small_ref[:, at * width : (at + 1) * width] += column_sum(total)
        grad_project = project_ref[own]
        yield
        grad_attended = dot_nt(output_weight_ref[...], grad_project)
        yield
        inners = []
        for head in range(HEADS):
            rows = slice(HALF * head, HALF * (head + 1))
            outs = outs_ref[own, rows, :]
            attended_ref[own, rows, :] = outs.astype(BF16)
            grads = grad_attended[rows].astype(BF16)
            grad_attended_ref[own, rows, :] = grads
            inners.append(column_sum(partial_sum(grads.astype(F32) * outs)))
            inner_ref[own, head : head + 1, :] = inners[-1]
        yield
        grad_attended = grad_attended_ref[own]
        add_to(weights_ref, dot(attended_ref[own], grad_project))
        grad_probs = dot(far_values, grad_attended)
        yield
        all_probs, all_grads = [], []
        for at in range(heights):
            probs_parts, grads_parts = [], []
            for head in range(HEADS):
                rows = slice(BLOCK * head, BLOCK * (head + 1))
                whole_rows = slice(HEADS * BLOCK * at + rows.start, HEADS * BLOCK * at + rows.stop)
                level = level_ref[own, head : head + 1, :]
                probs = jnp.exp(logits[at][rows] + far_bias[at] - level)
                probs_parts.append(probs.astype(BF16))
                grads_parts.append((probs * (grad_probs[whole_rows] - inners[head])).astype(BF16))
            all_probs.append(jnp.concatenate(probs_parts, axis=0))
            all_grads.append(jnp.concatenate(grads_parts, axis=0))
        yield
        all_spread = [dot(all_grads[at], spread_ref[at]).astype(BF16) for at in range(heights)]
        yield
        grad_queries = dot_tn(jnp.concatenate(far_keys, axis=0), jnp.concatenate(all_spread, axis=0))
        grad_queries_ref[own] = grad_queries.astype(BF16)
        wide_values = dot_nt(jnp.concatenate(all_probs, axis=0), grad_attended)
        yield
        grad_keys, grad_values = [], []
        for at in range(heights):
            rows = slice(HEADS * BLOCK * at, HEADS * BLOCK * (at + 1))
            grad_keys.append(of_heads(dot_nt(all_grads[at], coarse[at])))
            grad_values.append(of_heads(wide_values[rows]))
        grad_sums = jnp.concatenate(
            [
                jnp.concatenate(grad_keys, axis=0) * inverse,
                jnp.concatenate(grad_values, axis=0) * inverse,
            ],
            axis=1,
        )
        row = 0
        for piece in grad_pieces:
            rows = piece.shape[1]
            piece[own] = grad_sums[row : row + rows]
            row += rows

    interleaved(work, count)

    @pl.when(step == pl.num_programs(0) - 1)
    def _():
        split_rows(weights_ref, shard_ref[1], send_ref.at[0], keep_ref.at[0])


def near_back_kernel(
    begin,
    summing,
    lengths_ref,
    shard_ref,
    bits_ref,
    queries_ref,
    keys_ref,
    values_ref,
    grad_attended_ref,
    level_ref,
    inner_ref,
    spots_ref,
    spread_pair_ref,
    far_queries_ref,
    coarse_ref,
    pooled_keys_ref,
    pooled_values_ref,
    *refs,
):
    grad_queries_ref, grad_keys_ref, grad_values_ref, send_ref = refs[-4:]
    if summing:
        keep_ref, other_ref = refs[-6:-4]
        send_ref[...] = keep_ref[...] + other_ref[...]
    sequence = pl.program_id(0) + begin
    tok_count = keys_ref.shape[1]
    remaining = lengths_ref[sequence] - shard_ref[0] * tok_count
    inverse = coarse_inverse(remaining)
    keys = chunk_keys(keys_ref[0], pooled_keys_ref[0])
    values = chunk_keys(values_ref[0], pooled_values_ref[0])
    queries = queries_ref[0]
    grad_attended = grad_attended_ref[0]
    bias = [local_bias(remaining, chunk) for chunk in range(2)]
    coarse = coarse_ref[0]
    levels = [level_queries(queries, coarse, chunk) for chunk in range(2)]
    grad_keys, grad_values = {}, {}

    def products(unit):
        chunk, pair = unit
        lanes = slice(chunk * CHUNK, (chunk + 1) * CHUNK)
        tall = [block_diagonal(part[pair_of(pair)]) for part in levels[chunk]]
        tall_grads = block_diagonal(grad_attended[pair_of(pair), lanes])
        logits = local_logits(keys[chunk], tall, pair)
        return tall[0], tall_grads, logits, dot(values[chunk][:, pair_of(pair)], tall_grads)

    def slopes(unit, state):
        chunk, pair = unit
        lanes = slice(chunk * CHUNK, (chunk + 1) * CHUNK)
        tall, tall_grads, logits, grad_probs = state
        probs_sides, grads_sides = [], []
        for side in range(2):
            half = slice(side * CHUNK, (side + 1) * CHUNK)
            head = 2 * pair + side
            level = level_ref[0, head : head + 1, lanes]
            inner = inner_ref[0, head : head + 1, lanes]
            probs_parts, grads_parts = [], []
            for at in range(4):
                for rows in tiles(LOCAL_ROWS[at], min(LOCAL_ROWS[at], 2 * TILE)):
                    begin = LOCAL_STARTS[at] + rows.start
                    probs = jnp.exp(logits[at][rows, half] + bias[chunk][at][rows] - level)
                    grads = grad_probs[begin : begin + rows.stop - rows.start, half]
                    probs_parts.append(probs.astype(BF16))
                    grads_parts.append((probs * (grads - inner)).astype(BF16))
            probs_sides.append(jnp.concatenate(probs_parts, axis=0))
            grads_sides.append(jnp.concatenate(grads_parts, axis=0))
        return (
            tall,
            tall_grads,
            jnp.concatenate(probs_sides, axis=1),
            jnp.concatenate(grads_sides, axis=1),
        )

    def grads(unit, state):
        tall, tall_grads, probs, grad_logits = state
        grad_values[unit] = dot_nt(probs, tall_grads)
        return tall, grad_logits

    held = skewed(products, slopes, grads)
    for chunk in range(2):
        lanes = slice(chunk * CHUNK, (chunk + 1) * CHUNK)
        pairs = range(HEADS // 2)
        spread = []
        for at in range(1, 4):
            begin, rows = LOCAL_STARTS[at], LOCAL_ROWS[at]
            parts = [held[chunk, pair][1][begin : begin + rows] for pair in pairs]
            spread.append(
                dot(jnp.concatenate(parts, axis=0), spread_pair_ref[at - 1]).astype(BF16)
            )
        for pair in pairs:
            tall, grad_logits = held[chunk, pair]
            parts = [grad_logits[:CHUNK]] + [
                spread[at - 1][pair * LOCAL_ROWS[at] : (pair + 1) * LOCAL_ROWS[at]]
                for at in range(1, 4)
            ]
            evened = jnp.concatenate(parts, axis=0)
            grad_keys[chunk, pair] = dot_nt(evened, tall)
            wide = dot_tn(keys[chunk][:, pair_of(pair)], evened)
            total = diagonal_blocks(wide) + far_queries_ref[0, pair_of(pair), lanes].astype(F32)
            grad_queries_ref[0, pair_of(pair), lanes] = (total * 0.125).astype(BF16)

    def gathered(parts, begin, end):
        return [
            jnp.concatenate([parts[chunk, pair][begin:end] for pair in range(HEADS // 2)], axis=1)
            for chunk in range(2)
        ]

    fine_keys, coarse_keys = gathered(grad_keys, 0, CHUNK), gathered(grad_keys, CHUNK, LOCAL_KEYS)
    fine_values = gathered(grad_values, 0, CHUNK)
    coarse_values = gathered(grad_values, CHUNK, LOCAL_KEYS)
    inverse = four_times(inverse)
    for out_ref, fine, coarse in (
        (grad_keys_ref, fine_keys, coarse_keys),
        (grad_values_ref, fine_values, coarse_values),
    ):
        pooled = (jnp.concatenate(coarse, axis=0) * inverse).astype(BF16)
        total = jnp.concatenate(fine, axis=0) + dot(spots_ref[...], pooled)
        out_ref[0] = total.astype(out_ref.dtype)


def last_kernel(
    heights,
    piece_heights,
    lengths_ref,
    shard_ref,
    tokens_ref,
    grad_middle_ref,
    grad_queries_ref,
    grad_keys_ref,
    grad_values_ref,
    query_weight_ref,
    key_weight_ref,
    value_weight_ref,
    gain_ref,
    shift_ref,
    groups_ref,
    grad_up_bias_ref,
    small_middle_ref,
    *refs,
):
    pieces = refs[: len(piece_heights)]
    input_grad_ref, send_ref, keep_ref, weights_ref, small_ref, normed_ref, grads_ref = refs[-7:]
    sequence = pl.program_id(0)
    count, tok_count, width = tokens_ref.shape

    @pl.when(sequence == 0)
    def _():
        weights_ref[...] = jnp.zeros_like(weights_ref)
        small_ref[0:1, :] = grad_up_bias_ref[...]
        small_ref[1:2, :] = small_middle_ref[...]
        small_ref[2:, :] = jnp.zeros((small_ref.shape[0] - 2, small_ref.shape[1]), F32)

    gain, shift = gain_ref[...], shift_ref[...]
    for at in range(count):
        remaining = lengths_ref[sequence * count + at] - shard_ref[0] * tok_count
        far = [
            sum(piece[at] for piece, level in zip(pieces, piece_heights) if level == height)
            for height in range(heights)
        ]
        far = dot_tn(groups_ref[...], jnp.concatenate(far, axis=0).astype(BF16))
        grads_ref[at, :, :width] = grad_queries_ref[at].T
        for rows in tiles(tok_count):
            normed, _ = normalize(tokens_ref[at, rows].astype(F32))
            normed_ref[at, rows] = (normed * gain + shift).astype(BF16)
            valid = iota((TILE, width), 0) + rows.start < remaining
            keys = grad_keys_ref[at, rows].astype(F32) + far[rows, :width]
            values = grad_values_ref[at, rows].astype(F32) + far[rows, width:]
            keys = jnp.where(valid, keys, 0.0)
            values = jnp.where(valid, values, 0.0)
            grads_ref[at, rows, width : 2 * width] = keys.astype(BF16)
            grads_ref[at, rows, 2 * width :] = values.astype(BF16)
    grads = grads_ref[...].reshape(count * tok_count, 3 * width)
    grad_normed = (
        dot_nt(grads[:, :width], query_weight_ref[...])
        + dot_nt(grads[:, width : 2 * width], key_weight_ref[...])
        + dot_nt(grads[:, 2 * width :], value_weight_ref[...])
    )
    products = dot_tn(normed_ref[...].reshape(count * tok_count, width), grads)
    small = [0.0] * 4
    for at in range(count):
        for rows in tiles(tok_count):
            places = slice(at * tok_count + rows.start, at * tok_count + rows.stop)
            normed, scale = normalize(tokens_ref[at, rows].astype(F32))
            given = grad_normed[places]
            sums = [
                grads_ref[at, rows, :width].astype(F32),
                grads_ref[at, rows, 2 * width :].astype(F32),
                given * normed,
                given,
            ]
            small = [total + partial_sum(part) for total, part in zip(small, sums)]
            back = normalize_back(given * gain, normed, scale)
            input_grad_ref[at, rows] = grad_middle_ref[at, rows] + back
    for at, total in enumerate(small):
        small_ref[2:3, at * width : (at + 1) * width] += column_sum(total)
    for rows in tiles(width):
        weights_ref[rows, : 3 * width] += products[rows]

    @pl.when(sequence == pl.num_programs(0) - 1)
    def _():
        parts = small_ref.shape[1] // CHUNK
        for line in range(3):
            for part in range(parts):
                at = line * parts + part
                weights_ref[at : at + 1, 3 * width :] = small_ref[
                    line : line + 1, part * CHUNK : (part + 1) * CHUNK
                ]
        split_rows(weights_ref, shard_ref[1], send_ref.at[0], keep_ref.at[0])


def half_of(ref, bit):
    rows = ref.shape[1] // 2
    return ref[:, pl.ds(pl.multiple_of(bit * rows, 8), rows), :]


def first_sum_kernel(fetch, bits_ref, keep_ref, other_ref, token_ref, send_ref, next_ref, *scratch):
    rows = send_ref.shape[1]
    begin = pl.multiple_of((1 - bits_ref[1]) * rows, 8)
    fetched_ref, sems = scratch
    copies = []
    for at, ref in enumerate([keep_ref, other_ref][:fetch]):
        source = ref.at[:, pl.ds(begin, rows), :]
        copies.append(pltpu.make_async_copy(source, fetched_ref.at[at], sems.at[at]))
        copies[-1].start()
    for copy in copies:
        copy.wait()
    other = fetched_ref[1] if fetch > 1 else other_ref[:, pl.ds(begin, rows), :]
    send_ref[...] = fetched_ref[0] + other


def second_sum_kernel(
    fetch, bits_ref, keep_ref, other_ref, new_ref, token_ref, send_ref, stay_ref, next_ref, *scratch
):
    rows = new_ref.shape[1]
    half = rows // 2
    begin = pl.multiple_of(bits_ref[1] * rows, 8)
    fetched_ref, sems = scratch
    copies = []
    for at, ref in enumerate([keep_ref, other_ref][:fetch]):
        source = ref.at[:, pl.ds(begin, rows), :]
        copies.append(pltpu.make_async_copy(source, fetched_ref.at[at], sems.at[at]))
        copies[-1].start()
    for copy in copies:
        copy.wait()
    for out_ref, bit in ((send_ref, 1 - bits_ref[2]), (stay_ref, bits_ref[2])):
        offset = pl.multiple_of(bit * half, 8)
        part = pl.ds(offset, half)
        if fetch > 1:
            other = fetched_ref[1, :, part, :]
        else:
            other = other_ref[:, pl.ds(pl.multiple_of(begin + offset, 8), half), :]
        out_ref[...] = fetched_ref[0, :, part, :] + other + new_ref[:, part, :]


def split_sum_kernel(
    step, bits_ref, keep_ref, new_ref, token_ref, send_ref, stay_ref, next_ref
):
    bit = bits_ref[step]
    send_ref[...] = half_of(keep_ref, 1 - bit) + half_of(new_ref, 1 - bit)
    stay_ref[...] = half_of(keep_ref, bit) + half_of(new_ref, bit)


def last_sum_kernel(bits_ref, keep_ref, new_ref, token_ref, out_ref, next_ref):
    out_ref[...] = keep_ref[...] + new_ref[...]


def join_rows_kernel(step, bits_ref, own_ref, other_ref, token_ref, out_ref, next_ref):
    rows = own_ref.shape[1]
    bit = bits_ref[step]
    out_ref[:, pl.ds(pl.multiple_of(bit * rows, 8), rows), :] = own_ref[...]
    out_ref[:, pl.ds(pl.multiple_of((1 - bit) * rows, 8), rows), :] = other_ref[...]


def place_down_kernel(bits_ref, own_ref, other_ref, token_ref, out_ref, next_ref):
    rows = own_ref.shape[1]
    core = bits_ref[0]
    out_ref[pl.ds(pl.multiple_of(core * rows, 8), rows), :] = own_ref[0]
    out_ref[pl.ds(pl.multiple_of((1 - core) * rows, 8), rows), :] = other_ref[0]


def place_up_kernel(bits_ref, own_ref, other_ref, token_ref, up_ref, output_ref, next_ref):
    parts, rows, width = own_ref.shape
    core = bits_ref[0]
    for side in range(2):

        @pl.when(core == side)
        def _():
            for half, source in ((side, own_ref), (1 - side, other_ref)):
                for part in range(parts - 1):
                    column = (half * (parts - 1) // 2 + part // 2) * width
                    row = part % 2 * rows
                    up_ref[row : row + rows, column : column + width] = source[part]
                output_ref[half * rows : (half + 1) * rows, :] = source[parts - 1]


def place_last_kernel(vectors, bits_ref, own_ref, other_ref, token_ref, *refs):
    rows = own_ref.shape[1]
    core = bits_ref[0]
    outs, extra_ref = refs[:3], refs[-1]
    for half, source in ((core, own_ref), (1 - core, other_ref)):
        begin = pl.multiple_of(half * rows, 8)
        width = outs[0].shape[1]
        for at, out in enumerate(outs):
            out[pl.ds(begin, rows), :] = source[0, :, at * width : (at + 1) * width]
        extra_ref[pl.ds(begin, rows), :] = source[0, :, 3 * width :]
    row = 0
    for out in refs[3:-2]:
        for part in range(out.shape[1] // CHUNK):
            out[:, part * CHUNK : (part + 1) * CHUNK] = extra_ref[row : row + 1, :]
            row += 1


class Reducer:
    def __init__(self):
        self.shards = lax.axis_size("seq")
        self.batches = lax.axis_size("batch")
        seq_bits = self.shards.bit_length() - 1
        far_bits = self.batches.bit_length() - 2
        seq_half, far_half = seq_bits // 2, far_bits // 2
        orders = (
            [("seq", bit) for bit in range(seq_bits)]
            + [("batch", bit + 1) for bit in range(far_bits)],
            [("seq", (bit + seq_half) % seq_bits) for bit in range(seq_bits)]
            + [("batch", (bit + far_half) % far_bits + 1) for bit in range(far_bits)],
        )
        places = dict(seq=lax.axis_index("seq"), batch=lax.axis_index("batch"))
        core = places["batch"] & 1
        bits = [core]
        for first, second in zip(*orders):
            one, other = [(places[axis] >> bit) & 1 for axis, bit in (first, second)]
            bits.append(jnp.where(core == 0, one, other))
        self.steps = len(bits)
        self.token = None
        self.bits = jnp.stack(bits).astype(jnp.int32)
        self.pairs = [[] for _ in bits]
        for seq in range(self.shards):
            for batch in range(self.batches):
                moves = [("batch", 0)] + orders[batch & 1]
                for pairs, (axis, bit) in zip(self.pairs, moves):
                    to_seq = seq ^ (1 << bit) if axis == "seq" else seq
                    to_batch = batch ^ (1 << bit) if axis == "batch" else batch
                    pairs.append((seq * self.batches + batch, to_seq * self.batches + to_batch))

    def swap(self, array, step):
        return lax.ppermute(array, ("seq", "batch"), self.pairs[step])

    def run(self, kernel, name, in_specs, operands, out_specs, shapes, scratch=(), chunk=None, limit=32 * 2**20):
        anywhere = pl.BlockSpec(memory_space=pl.ANY)
        *outs, self.token = pl.pallas_call(
            kernel,
            in_specs=[pl.BlockSpec(memory_space=pltpu.SMEM)] + in_specs + [anywhere],
            out_specs=out_specs + [anywhere],
            out_shape=[jax.ShapeDtypeStruct(shape, F32) for shape in shapes + [TOKEN]],
            scratch_shapes=scratch,
            compiler_params=pltpu.CompilerParams(vmem_limit_bytes=limit),
            cost_estimate=pl.CostEstimate(
                flops=0, bytes_accessed=ROUND_BYTES[chunk], transcendentals=0
            ),
            name=name,
        )(self.bits, *operands, self.token)
        return outs

    def gate(self, name, *arrays):
        anywhere = pl.BlockSpec(memory_space=pl.ANY)
        *arrays, self.token = pl.pallas_call(
            lambda *refs: None,
            in_specs=[anywhere] * (len(arrays) + 1),
            out_specs=[anywhere] * (len(arrays) + 1),
            out_shape=[
                jax.ShapeDtypeStruct(shape, F32)
                for shape in [array.shape for array in arrays] + [TOKEN]
            ],
            input_output_aliases={at: at for at in range(len(arrays))},
            cost_estimate=pl.CostEstimate(flops=0, bytes_accessed=0, transcendentals=0),
            name=f"{name}_gate",
        )(*arrays, self.token)
        return arrays

    def total(self, name, terms, step, fetch):
        parts, full, width = terms[0].shape
        anywhere, vmem = pl.BlockSpec(memory_space=pl.ANY), pl.BlockSpec(memory_space=pltpu.VMEM)
        given = [anywhere] * fetch + [vmem] * (2 - fetch)
        if step <= 2:
            scratch = [
                pltpu.VMEM((fetch, parts, full // 2, width), F32),
                pltpu.SemaphoreType.DMA((fetch,)),
            ]
        if step == 1:
            kernel = functools.partial(first_sum_kernel, fetch)
            shapes = [(parts, full // 2, width)]
            (send,) = self.run(
                kernel, f"{name}_sum1", given, terms, [vmem], shapes, scratch, chunk=name
            )
            return send, terms
        if step == 2:
            kernel = functools.partial(second_sum_kernel, fetch)
            shapes = [(parts, full // 4, width)] * 2
            send, stay = self.run(
                kernel,
                f"{name}_sum2",
                given + [vmem],
                terms,
                [vmem] * 2,
                shapes,
                scratch,
                chunk=name,
                limit=VMEM_BYTES if fetch > 1 else 32 * 2**20,
            )
            return send, [stay]
        kernel = functools.partial(split_sum_kernel, step)
        shapes = [(parts, full // 2, width)] * 2
        send, stay = self.run(
            kernel, f"{name}_sum{step}", [vmem] * 2, terms, [vmem] * 2, shapes, chunk=name
        )
        return send, [stay]

    def finish(self, name, terms):
        vmem = pl.BlockSpec(memory_space=pltpu.VMEM)
        (out,) = self.run(
            last_sum_kernel, f"{name}_total", [vmem] * 2, terms, [vmem], [terms[0].shape], chunk=name
        )
        return out

    def join(self, name, own, other, step):
        parts, rows, width = own.shape
        vmem = pl.BlockSpec(memory_space=pltpu.VMEM)
        (out,) = self.run(
            functools.partial(join_rows_kernel, step),
            f"{name}_join{step}",
            [vmem, vmem],
            [own, other],
            [vmem],
            [(parts, 2 * rows, width)],
            chunk=name,
        )
        return out

    def place(self, name, kernel, own, other, shapes, scratch=()):
        vmem = pl.BlockSpec(memory_space=pltpu.VMEM)
        return self.run(
            kernel,
            f"{name}_place",
            [vmem, vmem],
            [own, other],
            [vmem] * len(shapes),
            shapes,
            scratch,
            chunk=name,
        )


class Chunk:
    def __init__(
        self,
        reducer,
        name,
        send,
        keep,
        kernel,
        shapes,
        scratch=(),
        gated=False,
        fetch=2,
    ):
        self.reducer, self.name = reducer, name
        self.last = reducer.steps - 1
        self.fits = keep.shape[1] >> self.last >= 8
        self.send, self.terms, self.gated, self.fetch = send, [keep], gated, fetch
        self.kernel, self.shapes, self.scratch = kernel, list(shapes), scratch
        self.outs = self.ready = None
        self.stages = self.run()

    def run(self):
        reducer, name, last = self.reducer, self.name, self.last
        if not self.fits:
            outs = reducer.place(
                name, self.kernel, self.terms[0], self.send, self.shapes, self.scratch
            )
            self.outs = lax.psum(outs, ("seq", "batch"))
            return
        if self.gated:
            (self.send,) = reducer.gate(name, self.send)
        self.terms = terms = self.terms + [reducer.swap(self.send, 0)]
        for step in range(1, last + 1):
            yield
            if step == 1 and self.ready is not None:
                send = self.ready
                if name == "down":
                    (send,) = reducer.gate(name, send)
            else:
                send, terms = reducer.total(name, terms, step, self.fetch)
            terms = terms + [reducer.swap(send, step)]
        yield
        block = reducer.finish(name, terms)
        for step in range(last, 0, -1):
            other = reducer.swap(block, step)
            yield
            block = reducer.join(name, block, other, step)
        other = reducer.swap(block, 0)
        yield
        self.outs = reducer.place(name, self.kernel, block, other, self.shapes, self.scratch)

    def first_sum(self, cuts):
        if not self.fits:
            return [], [], [pl.BlockSpec(TOKEN, lambda at, *_: (0, 0))], [(TOKEN, F32)]
        parts, full, width = self.terms[0].shape
        rows = full // 2
        block = (parts, rows // cuts, width)
        given = pl.BlockSpec(block, lambda at, *scalars: (0, (1 - scalars[2][1]) * cuts + at, 0))
        made = pl.BlockSpec(block, lambda at, *_: (0, at, 0))
        return self.terms, [given] * 2, [made], [((parts, rows, width), F32)]

    def forward(self):
        return next(self.stages, self) is not self


def by_sequence(*shape, begin=0, count=1):
    return pl.BlockSpec((count,) + shape, lambda at, *_: (at + begin,) + (0,) * len(shape))


def whole(*shape):
    return pl.BlockSpec(shape, lambda at, *_: (0,) * len(shape))


def call(
    reducer,
    kernel,
    grid,
    in_specs,
    out_specs,
    out_shapes,
    flops,
    operands,
    aliases=None,
    scratch=(),
    prefetch=2,
):
    anywhere = pl.BlockSpec(memory_space=pl.ANY)
    given, made = len(in_specs), len(out_specs)
    tokens = [] if reducer.token is None else [reducer.token]

    def body(*refs):
        inputs = refs[: prefetch + given]
        rest = refs[prefetch + given + len(tokens) :]
        kernel(*inputs, *rest[:made], *rest[made + 1 :])

    *outs, reducer.token = pl.pallas_call(
        body,
        grid_spec=pltpu.PrefetchScalarGridSpec(
            num_scalar_prefetch=prefetch,
            grid=grid,
            in_specs=in_specs + [anywhere] * len(tokens),
            out_specs=out_specs + [anywhere],
            scratch_shapes=scratch,
        ),
        out_shape=[
            jax.ShapeDtypeStruct(shape, dtype) for shape, dtype in out_shapes + [(TOKEN, F32)]
        ],
        input_output_aliases=aliases or {},
        compiler_params=pltpu.CompilerParams(
            dimension_semantics=("arbitrary",), vmem_limit_bytes=VMEM_BYTES
        ),
        cost_estimate=pl.CostEstimate(flops=flops, bytes_accessed=20_000_000, transcendentals=0),
    )(*operands, *tokens)
    return outs


def local(
    tokens,
    lengths,
    query_weight,
    key_weight,
    value_weight,
    output_weight,
    up_weight,
    down_weight,
    query_bias,
    value_bias,
    output_bias,
    up_bias,
    down_bias,
    first_gain,
    first_shift,
    second_gain,
    second_shift,
    cotangent,
):
    seq_count, tok_count, width = tokens.shape
    inner_width = up_weight.shape[1]
    shards = lax.axis_size("seq")
    shard_index = lax.axis_index("seq")
    heights = shards.bit_length() - 1
    grid = (seq_count,)
    reducer = Reducer()
    core = reducer.bits[:1]
    shard = jnp.stack([shard_index.astype(jnp.int32), reducer.bits[0]])

    def row(vector):
        return vector.reshape(1, -1)

    groups = []
    for height in range(heights):
        members = group_members(tok_count, BLOCK << height)
        groups.append(np.pad(members, ((0, max(8 - members.shape[0], 0)), (0, 0))))
    groups = jnp.asarray(np.concatenate(groups, axis=0), BF16)
    members = jnp.asarray(coarse_members(tok_count), BF16)
    spots = jnp.asarray(coarse_members(tok_count).T, BF16)
    near_spread = jnp.asarray(np.concatenate([averaging(at) for at in range(1, 4)], axis=1), BF16)
    near_pair = jnp.asarray(np.stack([averaging_pair(at) for at in range(1, 4)]), BF16)
    far_pair = jnp.asarray(np.stack([averaging_pair(4 + at) for at in range(heights)]), BF16)

    fine = by_sequence(tok_count, width)
    tall = by_sequence(width, tok_count)
    heads = by_sequence(HEADS, tok_count)
    square = whole(width, width)
    vector = whole(1, width)
    fine_shape = (seq_count, tok_count, width)
    tall_shape = (seq_count, width, tok_count)
    heads_shape = (seq_count, HEADS, tok_count)
    sum_shapes = [(BLOCK >> height, 2 * width) for height in range(heights)]
    together = 2 - seq_count % 2
    some_fine = by_sequence(tok_count, width, count=together)
    some_tall = by_sequence(width, tok_count, count=together)
    queries, keys, values, *sums = call(
        reducer,
        functools.partial(project_kernel, heights),
        (seq_count // together,),
        [some_fine, square, square, square, vector, vector, vector, vector, whole(*groups.shape)],
        [some_tall, some_fine, some_fine]
        + [by_sequence(*shape, count=together) for shape in sum_shapes],
        [(tall_shape, BF16), (fine_shape, BF16), (fine_shape, BF16)]
        + [((seq_count,) + shape, F32) for shape in sum_shapes],
        2 * seq_count * tok_count * width * width * 3,
        scratch=[pltpu.VMEM((together, tok_count, width), BF16)] * 2,
        operands=[lengths,
        shard,
        tokens,
        query_weight,
        key_weight,
        value_weight,
        row(query_bias),
        row(value_bias),
        row(first_gain),
        row(first_shift),
        groups],
    )

    def swap(array, mask):
        return lax.ppermute(array, "seq", [(at, at ^ mask) for at in range(shards)])

    received = [swap(sums[mask.bit_length() - 1], mask) for mask in range(1, shards)]
    pieces = received[:3]
    for height in range(2, heights):
        pieces.append(
            jnp.concatenate(received[(1 << height) - 1 : (2 << height) - 1], axis=1)
        )
    piece_shapes = [piece.shape[1:] for piece in pieces]
    piece_specs = [by_sequence(*shape, count=together) for shape in piece_shapes]

    spread_shape = (seq_count, width, 2 * near_spread.shape[1])
    pool_shape = (seq_count, members.shape[0], width)
    spread_block, pool_block = by_sequence(*spread_shape[1:]), by_sequence(*pool_shape[1:])
    maxima, totals, numer, near_queries, pooled_near_keys, pooled_near_values = call(
        reducer,
        near_kernel,
        grid,
        [tall, fine, fine, whole(*members.shape), whole(*near_spread.shape)],
        [heads, heads, tall, spread_block, pool_block, pool_block],
        [
            (heads_shape, F32),
            (heads_shape, F32),
            (tall_shape, BF16),
            (spread_shape, BF16),
            (pool_shape, BF16),
            (pool_shape, BF16),
        ],
        1_000_000_000,
        [lengths, shard, queries, keys, values, members, near_spread],
    )

    some_heads = by_sequence(HEADS, tok_count, count=together)
    middle, second, outs, level, all_far_queries = call(
        reducer,
        functools.partial(join_kernel, heights, shards, len(pieces)),
        (seq_count // together,),
        [
            some_fine,
            some_tall,
            some_heads,
            some_heads,
            some_tall,
            square,
            vector,
            vector,
            vector,
            whole(*far_pair.shape),
        ]
        + [pl.BlockSpec(memory_space=pltpu.VMEM)] * len(pieces),
        [some_fine, some_fine, some_tall, some_heads]
        + [by_sequence(width, heights * tok_count, count=together)],
        [
            (fine_shape, F32),
            (fine_shape, BF16),
            (tall_shape, F32),
            (heads_shape, F32),
            ((seq_count, width, heights * tok_count), BF16),
        ],
        2 * seq_count * tok_count * width * width,
        scratch=[pltpu.VMEM((together, width, tok_count), BF16)],
        operands=[lengths,
        shard,
        tokens,
        queries,
        maxima,
        totals,
        numer,
        output_weight,
        row(output_bias),
        row(second_gain),
        row(second_shift),
        far_pair,
        *pieces],
    )

    steps = inner_width // width
    half_steps = steps // 2
    all_rows = whole(*fine_shape)

    def turned(at, core):
        return lax.rem(at + half_steps * (1 - core[0]), steps)

    columns = pl.BlockSpec((width, width), lambda at, core: (0, turned(at, core)))
    column_row = pl.BlockSpec((1, width), lambda at, core: (0, turned(at, core)))
    blocks = pl.BlockSpec((width, width), lambda at, core: (turned(at, core), 0))
    rows_count = seq_count * tok_count
    half_width = width // 2
    parts = steps + 1

    def halves(block, axis):
        def place(at):
            return tuple(at if place == axis else 0 for place in range(3))

        return [
            pl.BlockSpec(block, lambda at, core: place(jnp.minimum(at, half_steps - 1))),
            pl.BlockSpec(block, lambda at, core: place(jnp.maximum(at - half_steps, 0))),
        ]

    grad_second, down_send, down_keep, up_send, up_keep, grad_up_bias, hidden = call(
        reducer,
        functools.partial(hidden_kernel, steps),
        (steps,),
        [all_rows, all_rows, columns, blocks, column_row],
        [all_rows]
        + halves((1, width, width), 1)
        + halves((2, half_width, width), 0)
        + [column_row, pl.BlockSpec((rows_count, width), lambda at, core: (0, turned(at, core)))],
        [
            (fine_shape, BF16),
            ((1, inner_width // 2, width), F32),
            ((1, inner_width // 2, width), F32),
            ((parts, half_width, width), F32),
            ((parts, half_width, width), F32),
            ((1, inner_width), F32),
            ((rows_count, inner_width), BF16),
        ],
        2 * rows_count * width * 5 * inner_width,
        [core, second, cotangent, up_weight, down_weight, row(up_bias)],
        scratch=[
            pltpu.VMEM(fine_shape, F32),
            pltpu.VMEM((width, rows_count), BF16),
            pltpu.VMEM((rows_count, width), BF16),
        ],
        prefetch=1,
    )
    chunk_down = Chunk(
        reducer,
        "down",
        down_send,
        down_keep,
        place_down_kernel,
        [(inner_width, width)],
    )
    chunk_down.forward()

    grad_middle, grad_attended, inner_sums, far_queries, *rest = call(
        reducer,
        functools.partial(backward_kernel, heights, shards, len(pieces)),
        (seq_count // together,),
        [
            some_fine,
            by_sequence(width, heights * tok_count, count=together),
            some_fine,
            some_tall,
            some_heads,
            some_fine,
            square,
            vector,
            whole(*far_pair.shape),
        ]
        + [pl.BlockSpec(memory_space=pltpu.VMEM)] * len(pieces)
        + [pl.BlockSpec(memory_space=pl.ANY)] * 2,
        [some_fine, some_tall, some_heads, some_tall]
        + piece_specs
        + [pl.BlockSpec((1, half_width, width), lambda at, *_: (parts - 1, 0, 0))] * 2
        + [whole(1, inner_width)],
        [
            (fine_shape, F32),
            (tall_shape, BF16),
            (heads_shape, F32),
            (tall_shape, BF16),
        ]
        + [((seq_count,) + shape, F32) for shape in piece_shapes]
        + [((parts, half_width, width), F32)] * 2
        + [((1, inner_width), F32)],
        2 * rows_count * width * 2 * width,
        [lengths,
        shard,
        cotangent,
        all_far_queries,
        middle,
        outs,
        level,
        grad_second,
        output_weight,
        row(second_gain),
        far_pair,
        *pieces,
        up_send,
        up_keep],
        aliases={
            11 + len(pieces): 4 + len(pieces),
            12 + len(pieces): 5 + len(pieces),
        },
        scratch=[
            pltpu.VMEM((width, width), F32),
            pltpu.VMEM((together, tok_count, width), BF16),
            pltpu.VMEM((together, width, tok_count), BF16),
        ],
    )
    grad_pieces = rest[: len(pieces)]
    up_send, up_keep, small_middle = rest[len(pieces) :]
    chunk_up = Chunk(
        reducer,
        "up",
        up_send,
        up_keep,
        place_up_kernel,
        [(width, inner_width), (width, width)],
    )
    turns, layer = dict(d=chunk_down, u=chunk_up), []

    def take(place):
        for turn in ROUNDS.split(",")[place]:
            if turn == "o":
                layer.extend(
                    call(
                        reducer,
                        output_kernel,
                        grid,
                        [
                            pl.BlockSpec((tok_count, inner_width), lambda at, *_: (at, 0)),
                            fine,
                            whole(inner_width, width),
                            vector,
                        ],
                        [fine],
                        [(fine_shape, BF16)],
                        2 * rows_count * width * inner_width,
                        [core, hidden, middle, down_weight, row(down_bias)],
                        prefetch=1,
                    )
                )
            else:
                turns[turn].forward()

    returned = []
    for mask in range(1, shards):
        height = mask.bit_length() - 1
        if height < 2:
            piece = grad_pieces[mask - 1]
        else:
            rows = BLOCK >> height
            begin = (mask - (1 << height)) * rows
            piece = grad_pieces[height + 1][:, begin : begin + rows]
        returned.append(swap(piece, mask))
    take(0)
    half = seq_count // 2
    near_grads = ()
    anywhere = pl.BlockSpec(memory_space=pl.ANY)
    for begin in (0, half):
        some = functools.partial(by_sequence, begin=begin)
        some_fine, some_tall = some(tok_count, width), some(width, tok_count)
        some_heads = some(HEADS, tok_count)
        in_specs = [
            some_tall,
            some_fine,
            some_fine,
            some_tall,
            some_heads,
            some_heads,
            whole(*spots.shape),
            whole(*near_pair.shape),
            some_tall,
            some(*spread_shape[1:]),
            some(*pool_shape[1:]),
            some(*pool_shape[1:]),
        ]
        chunk = chunk_up if begin else chunk_down
        terms, sum_in, sum_out, sum_shape = chunk.first_sum(half)
        *near_grads, send = call(
            reducer,
            functools.partial(near_back_kernel, begin, len(terms) > 0),
            (half,),
            in_specs + [anywhere] * len(near_grads) + sum_in,
            [some_tall, some_fine, some_fine] + sum_out,
            [(tall_shape, BF16), (fine_shape, F32), (fine_shape, BF16)] + sum_shape,
            2_000_000_000,
            [
                lengths,
                shard,
                reducer.bits,
                queries,
                keys,
                values,
                grad_attended,
                level,
                inner_sums,
                spots,
                near_pair,
                far_queries,
                near_queries,
                pooled_near_keys,
                pooled_near_values,
                *near_grads,
                *terms,
            ],
            {3 + len(in_specs) + at: at for at in range(len(near_grads))},
            prefetch=3,
        )
        chunk.ready = send
        if begin == 0:
            returned = reducer.gate("far", *returned)
            take(1)
    take(2)

    back_pieces, back_heights = [], []
    for mask in range(1, shards):
        height = mask.bit_length() - 1
        if height < 2:
            back_pieces.append(returned[mask - 1])
            back_heights.append(height)
    for height in range(2, heights):
        total = sum(returned[(1 << height) - 1 : (2 << height) - 1])
        back_pieces.append(jnp.pad(total, ((0, 0), (0, 8 - total.shape[1]), (0, 0))))
        back_heights.append(height)
    some_fine = by_sequence(tok_count, width, count=together)
    some_tall = by_sequence(width, tok_count, count=together)
    input_grad, last_send, last_keep = call(
        reducer,
        functools.partial(last_kernel, heights, tuple(back_heights)),
        (seq_count // together,),
        [
            some_fine,
            some_fine,
            some_tall,
            some_fine,
            some_fine,
            square,
            square,
            square,
            vector,
            vector,
            whole(*groups.shape),
            whole(1, inner_width),
            whole(1, inner_width),
        ]
        + [by_sequence(*piece.shape[1:], count=together) for piece in back_pieces],
        [some_fine] + [whole(1, half_width, 3 * width + CHUNK)] * 2,
        [(fine_shape, F32)] + [((1, half_width, 3 * width + CHUNK), F32)] * 2,
        2 * seq_count * tok_count * width * width * 6,
        [lengths,
        shard,
        tokens,
        grad_middle,
        *near_grads,
        query_weight,
        key_weight,
        value_weight,
        row(first_gain),
        row(first_shift),
        groups,
        grad_up_bias,
        small_middle,
        *back_pieces],
        scratch=[
            pltpu.VMEM((width, 3 * width + CHUNK), F32),
            pltpu.VMEM((8, inner_width), F32),
            pltpu.VMEM((together, tok_count, width), BF16),
            pltpu.VMEM((together, tok_count, 3 * width), BF16),
        ],
    )
    vectors = [inner_width] + [width] * 8
    chunk_last = Chunk(
        reducer,
        "last",
        last_send,
        last_keep,
        functools.partial(place_last_kernel, vectors),
        [(width, width)] * 3 + [(1, length) for length in vectors],
        [pltpu.VMEM((width, CHUNK), F32)],
        gated=True,
        fetch=1,
    )
    turns["l"] = chunk_last
    take(3)
    for chunk in turns.values():
        while chunk.forward():
            pass
    grad_query, grad_key, grad_value, *vectors = chunk_last.outs
    (grad_down,) = chunk_down.outs
    grad_up, grad_output = chunk_up.outs
    (
        grad_up_bias,
        grad_down_bias,
        grad_second_gain,
        grad_second_shift,
        grad_output_bias,
        grad_query_bias,
        grad_value_bias,
        grad_first_gain,
        grad_first_shift,
    ) = [vector.reshape(-1) for vector in vectors]
    return (
        layer[0],
        input_grad,
        grad_query,
        grad_key,
        grad_value,
        grad_output,
        grad_up,
        grad_down,
        grad_query_bias,
        grad_value_bias,
        grad_output_bias,
        grad_up_bias,
        grad_down_bias,
        grad_first_gain,
        grad_first_shift,
        grad_second_gain,
        grad_second_shift,
    )


def solution(mesh):
    rows = P("batch", "seq", None)
    return jax.shard_map(
        local,
        mesh=mesh,
        in_specs=(rows, P("batch")) + (P(),) * 15 + (rows,),
        out_specs=(rows, rows) + (P(),) * 15,
        check_vma=False,
    )
```

time: 1040 us -> 249 us (0.24)
  local copies, waits for them, and re-layouts: 515 us -> 7.63 us
  other arithmetic: 157 us -> 0.59 us
  matrix products: 155 us -> 0 us
  Pallas kernels: 0 us -> 121 us
  waiting for transfers between devices: 132 us -> 73.1 us
  blocking collectives: 50.9 us -> 0 us
  starting transfers between devices: 0.53 us -> 44.3 us
  between operations: 18.4 us -> 1.33 us
    reshape x93 -> x0, local copies, waits for them, and re-layouts: 198 us -> none  [the longest x50 113 us: spread_rows(): return widened.reshape((leading[0], leading[1] * factor) + array.shape[2:])]
    dot_general x54 -> x0, matrix products: 155 us -> none  [the longest x15 35.8 us: coarse_attend(): jnp.einsum('sbqhd,sbkhd->sbqhk', query_means, key_means, precision=HIGHEST)]
    psum x1 -> x0, waiting for transfers between devices: 132 us -> none  [local(): lax.psum((grad_query_weight, grad_key_weight, grad_value_weight, grad_out...]
    pallas_call x0 -> x40, Pallas kernels: none -> 121 us  [the longest x9 89 us: call(): pl.pallas_call(body, grid_spec=pltpu.PrefetchScalarGridSpec(num_scalar_pr...]
    reduce_sum x44 -> x0, other arithmetic: 97.1 us -> none  [the longest x23 70.4 us: collapse_rows(): jnp.sum(array.reshape((array.shape[0], array.shape[1] // factor, factor)...]
    another operation x31 -> x1, local copies, waits for them, and re-layouts: 74.5 us -> 0.6 us  [__init__(): self.bits = jnp.stack(bits).astype(jnp.int32)]
    ppermute x0 -> x36, waiting for transfers between devices: none -> 73.1 us  [the longest x30 72.5 us: swap(): return lax.ppermute(array, ('seq', 'batch'), self.pairs[step])]
    broadcast_in_dim x86 -> x0, local copies, waits for them, and re-layouts: 61.1 us -> none  [the longest x82 60.9 us: spread_rows(): jnp.broadcast_to(array[:, :, None], leading + (factor,) + array.shape[2:])]
  transfers between devices with their start and end apart: 3 -> 36, of which waited for: 1 -> 17; matrix products, arithmetic and copies ran while one was open for 40% -> 0% of each run, Pallas kernels for 0% -> 33%
where the time goes in v1:
time: 249 us; the launch traced here: 248 us
  Pallas kernels  121 us (49%)
  waiting for transfers between devices  73.1 us (29%)
  starting transfers between devices  44.3 us (18%)
  local copies, waits for them, and re-layouts  7.63 us (3%)
    pallas_call x9, Pallas kernels, call(): pl.pallas_call(body, grid_spec=pltpu.PrefetchScalarGridSpec(num_scalar_pr...  89 us
    ppermute x30, waiting for transfers between devices, swap(): return lax.ppermute(array, ('seq', 'batch'), self.pairs[step])  72.5 us
    ppermute x30, starting transfers between devices, swap(): return lax.ppermute(array, ('seq', 'batch'), self.pairs[step])  36.3 us
    pallas_call x28, Pallas kernels, run(): pl.pallas_call(kernel, in_specs=[pl.BlockSpec(memory_space=pltpu.SMEM)] +...  32 us
    ppermute x6, starting transfers between devices, swap(): return lax.ppermute(array, 'seq', [(at, at ^ mask) for at in range(shards)])  8.01 us
    unnamed x38, local copies, waits for them, and re-layouts  7.04 us
  transfers between devices with their start and end apart: 36, of which 17 were waited for; matrix products, arithmetic and copies ran while one was open for 0% of the time, Pallas kernels for 33%

profile of v1, /device:TPU:0, one launch (start us, length us, event | category | flops | bytes accessed | tf_op | source)
XLA Modules:
  0.0 247.9 jit_solution(9155491864189509375)
XLA Ops:
  1.2 5.9 %shard_map.359 = (bf16[4,512,256]{2,1,0:T(8,128)(2,1)}, bf16[4,256,512]{2,1,0:T(8,128)(2,1)}, bf16[4,256,512]{2,1,0:T(8,128)(2,1)}, f32[4,16,1024]{2,1,0:T(8,128...) custom-call(s32[4]{0:T(128)} %refs_0_.13, s32[2]{0:T(128)} %pad_add_fusion.refs_1_, bf16[4,256,512]{2,1,0:T(8,128)(2,1)} %refs_2_.9, ...), custom_call_target="tpu_custom_call" | custom-call | flops 1610612736 | bytes 20000000 | tf_op jit(solution)/shard_map/pallas_call | solution.py:1238
  7.1 3.0 %collective-permute-start = (f32[4,16,1024]{2,1,0:T(8,128)}, f32[4,16,1024]{2,1,0:T(8,128)S(1)}, u32[]{:S(2)}, u32[]{:S(2)}) collective-permute-start(f32[4,16,1024]{2,1,0:T(8,128)} %get-tuple-element.162), channel_id=1, source_target_pairs={{0,8},{8,0},{16,24},{24,16},{1,9},{9,1},{17,25},{25,17},{2,10},{10... | collective-permute-start | bytes 786440 | tf_op jit(solution)/shard_map/ppermute | solution.py:1340
  10.1 1.5 collective-permute-start.2
  11.6 8.5 %shard_map.360 = (f32[4,8,256]{2,1,0:T(8,128)}, f32[4,8,256]{2,1,0:T(8,128)}, bf16[4,512,256]{2,1,0:T(8,128)(2,1)}, bf16[4,512,768]{2,1,0:T(8,128)(2,1)}, bf16[4...) custom-call(s32[4]{0:T(128)} %refs_0_.13, s32[2]{0:T(128)} %pad_add_fusion.refs_1_, ...), custom_call_target="tpu_custom_call" | custom-call | flops 1000000000 | bytes 20000000 | tf_op jit(solution)/shard_map/pallas_call | solution.py:1238
  21.4 7.6 %shard_map.361 = (f32[4,256,512]{2,1,0:T(8,128)}, bf16[4,256,512]{2,1,0:T(8,128)(2,1)}, f32[4,512,256]{2,1,0:T(8,128)}, f32[4,8,256]{2,1,0:T(8,128)}, bf16[4,512,512]{2,1,0:T(8,128)(2,1)}, /*index=5*/f32[8,128]{1,0:T(8,128)}) custom-call(s32[4]{0:T(128)} %refs_0_.13, s32[2]{0:T(128)} %pad_add_fusion.refs_1_, bf16[4,256,512]{2,1,0:T(8,128)(2,1)} %refs_2_.9, ...), custom_call_target="tpu_custom_call" | custom-call | flops 536870912 | bytes 20000000 | tf_op jit(solution)/shard_map/pallas_call | solution.py:1238
  29.0 20.2 %shard_map.362 = (bf16[4,256,512]{2,1,0:T(8,128)(2,1)}, f32[1,1024,512]{2,1,0:T(8,128)}, f32[1,1024,512]{2,1,0:T(8,128)}, f32[5,256,512]{2,1,0:T(8,128)}, f32[5,...) custom-call(s32[1]{0:T(128)} %bitcast.refs_0_, ...), custom_call_target="tpu_custom_call" | custom-call | flops 10737418240 | bytes 20000000 | tf_op jit(solution)/shard_map/pallas_call | solution.py:1238
  49.2 10.8 %shard_map.363 = (f32[4,256,512]{2,1,0:T(8,128)}, bf16[4,512,256]{2,1,0:T(8,128)(2,1)}, f32[4,8,256]{2,1,0:T(8,128)}, bf16[4,512,256]{2,1,0:T(8,128)(2,1)}, f32[...) custom-call(s32[4]{0:T(128)} %refs_0_.13, ...), custom_call_target="tpu_custom_call", output_to_operand_aliasing={{7}: (14, {}), {8}: (15, {})} | custom-call | flops 1073741824 | bytes 20000000 | tf_op jit(solution)/shard_map/pallas_call | solution.py:1238
  60.6 1.5 collective-permute-start.5
  62.7 1.5 collective-permute-start.6
  64.7 9.0 %shard_map.364 = (bf16[4,512,256]{2,1,0:T(8,128)(2,1)}, f32[4,256,512]{2,1,0:T(8,128)}, bf16[4,256,512]{2,1,0:T(8,128)(2,1)}, f32[1,512,512]{2,1,0:T(8,128)}, f32[8,128]{1,0:T(8,128)}) custom-call(s32[4]{0:T(128)} %refs_0_.13, s32[2]{0:T(128)} %pad_add_fusion.refs_1_, s32[5]{0:T(128)} %stack.31.refs_2_.bits_ref, ...), custom_call_target="tpu_custom_call" | custom-call | flops 2000000000 | bytes 20000000 | tf_op jit(solution)/shard_map/pallas_call | solution.py:1238
  74.5 1.5 collective-permute-start.9
  76.0 8.6 %shard_map.365 = (bf16[4,512,256]{2,1,0:T(8,128)(2,1)}, f32[4,256,512]{2,1,0:T(8,128)}, bf16[4,256,512]{2,1,0:T(8,128)(2,1)}, f32[5,128,512]{2,1,0:T(8,128)}, f32[8,128]{1,0:T(8,128)}) custom-call(s32[4]{0:T(128)} %refs_0_.13, s32[2]{0:T(128)} %pad_add_fusion.refs_1_, ...), custom_call_target="tpu_custom_call", output_to_operand_aliasing={{0}: (15, {}), {1}: (16, {}), {2}: (17, {})} | custom-call | flops 2000000000 | bytes 20000000 | tf_op jit(solution)/shard_map/pallas_call | solution.py:1238
  85.2 4.3 %collective-permute-done.9.new_ref = f32[1,512,512]{2,1,0:T(8,128)S(1)} collective-permute-done((f32[1,512,512]{2,1,0:T(8,128)}, f32[1,512,512]{2,1,0:T(8,128)S(1)}, u32[]{:S(2)}, u32[]{:S(2)}) %collective-permute-start.9) | collective-permute-done | bytes 1048608 | tf_op jit(solution)/shard_map/ppermute | solution.py:1036
  90.5 3.9 %down_sum2.1 = (f32[1,256,512]{2,1,0:T(8,128)}, f32[1,256,512]{2,1,0:T(8,128)}, f32[8,128]{1,0:T(8,128)}) custom-call(s32[5]{0:T(128)} %stack.31.refs_2_.bits_ref, f32[1,1024,512]{2,1,0:T(8,128)} %get-tuple-element.184.refs_15_.keep_ref, f32[1,1024,512]{2,1,0:T(8,128)} %collective-permute-done.4.refs_16_.other_ref, f32[1,512,512]{2,1,0:T(8,128)} %copy-done.13, ...), custom_call_target="tpu_custom_call" | custom-call | bytes 40000000 | tf_op jit(solution)/shard_map/down_sum2/pallas_call | solution.py:1040
  94.4 1.5 collective-permute-start.10
  95.9 12.0 %shard_map.366 = (f32[4,256,512]{2,1,0:T(8,128)}, f32[1,256,1664]{2,1,0:T(8,128)}, f32[1,256,1664]{2,1,0:T(8,128)}, f32[8,128]{1,0:T(8,128)}) custom-call(s32[4]{0:T(128)} %refs_0_.13, s32[2]{0:T(128)} %pad_add_fusion.refs_1_, bf16[4,256,512]{2,1,0:T(8,128)(2,1)} %refs_2_.9, f32[4,256,512]{2,1,0:T(8,128)} %get-tuple-element.202.refs_3_, ...), custom_call_target="tpu_custom_call" | custom-call | flops 3221225472 | bytes 20000000 | tf_op jit(solution)/shard_map/pallas_call | solution.py:1238
  109.8 1.6 collective-permute-start.12
  111.4 4.3 %up_sum2.1 = (f32[5,64,512]{2,1,0:T(8,128)}, f32[5,64,512]{2,1,0:T(8,128)}, f32[8,128]{1,0:T(8,128)}) custom-call(s32[5]{0:T(128)} %stack.31.refs_2_.bits_ref, f32[5,256,512]{2,1,0:T(8,128)} %get-tuple-element.176.refs_18_.keep_ref, f32[5,256,512]{2,1,0:T(8,128)} %collective-permute-done.3.refs_19_.other_ref, f32[5,128,512]{2,1,0:T(8,128)} %collective-permute-done.8.new_ref, ...), custom_call_target="tpu_custom_call" | custom-call | bytes 40000000 | tf_op jit(solution)/shard_map/up_sum2/pallas_call | solution.py:1040
  115.8 1.6 collective-permute-done.12.new_ref
  119.9 1.5 collective-permute-start.11
  121.4 2.3 collective-permute-start.14
  123.7 3.6 %collective-permute-done.14.new_ref = f32[1,64,512]{2,1,0:T(8,128)S(1)} collective-permute-done((f32[1,64,512]{2,1,0:T(8,128)S(1)}, f32[1,64,512]{2,1,0:T(8,128)S(1)}, u32[]{:S(2)}, u32[]{:S(2)}) %collective-permute-start.14) | collective-permute-done | bytes 131104 | tf_op jit(solution)/shard_map/ppermute | solution.py:1036
  129.4 1.5 collective-permute-start.19
  131.6 2.1 collective-permute-start.15
  133.7 3.1 %collective-permute-start.17 = (f32[1,64,512]{2,1,0:T(8,128)S(1)}, f32[1,64,512]{2,1,0:T(8,128)S(1)}, u32[]{:S(2)}, u32[]{:S(2)}) collective-permute-start(f32[1,64,512]{2,1,0:T(8,128)S(1)} %get-tuple-element.233.own_ref), channel_id=1, source_target_pairs={{0,4},{1,3},{2,6},{3,1},{4,0},{5,7},{6,2},{7,5},{8,12},{9,11},{10,... | collective-permute-start | bytes 393224 | tf_op jit(solution)/shard_map/ppermute | solution.py:1036
  136.8 7.9 %collective-permute-done.15.new_ref = f32[5,32,512]{2,1,0:T(8,128)S(1)} collective-permute-done((f32[5,32,512]{2,1,0:T(8,128)S(1)}, f32[5,32,512]{2,1,0:T(8,128)S(1)}, u32[]{:S(2)}, u32[]{:S(2)}) %collective-permute-start.15) | collective-permute-done | bytes 327712 | tf_op jit(solution)/shard_map/ppermute | solution.py:1036
  147.8 1.5 collective-permute-start.18
  149.3 5.6 %collective-permute-done.20.new_ref = f32[1,64,1664]{2,1,0:T(8,128)S(1)} collective-permute-done((f32[1,64,1664]{2,1,0:T(8,128)S(1)}, f32[1,64,1664]{2,1,0:T(8,128)S(1)}, u32[]{:S(2)}, u32[]{:S(2)}) %collective-permute-start.20) | collective-permute-done | bytes 426016 | tf_op jit(solution)/shard_map/ppermute | solution.py:1036
  156.6 1.5 collective-permute-start.22
  158.1 1.8 collective-permute-start.16
  159.9 2.5 %collective-permute-start.23 = (f32[1,32,1664]{2,1,0:T(8,128)S(1)}, f32[1,32,1664]{2,1,0:T(8,128)S(1)}, u32[]{:S(2)}, u32[]{:S(2)}) collective-permute-start(f32[1,32,1664]{2,1,0:T(8,128)S(1)} %get-tuple-element.246), channel_id=1, source_target_pairs={{0,2},{1,5},{2,0},{3,7},{4,6},{5,1},{6,4},{7,3},{8,10},{9,13},{10,... | collective-permute-start | bytes 638984 | tf_op jit(solution)/shard_map/ppermute | solution.py:1036
  162.4 6.0 %collective-permute-done.16.new_ref = f32[5,16,512]{2,1,0:T(8,128)S(1)} collective-permute-done((f32[5,16,512]{2,1,0:T(8,128)S(1)}, f32[5,16,512]{2,1,0:T(8,128)S(1)}, u32[]{:S(2)}, u32[]{:S(2)}) %collective-permute-start.16) | collective-permute-done | bytes 163872 | tf_op jit(solution)/shard_map/ppermute | solution.py:1036
  170.5 11.1 %collective-permute-done.21.other_ref = f32[5,16,512]{2,1,0:T(8,128)S(1)} collective-permute-done((f32[5,16,512]{2,1,0:T(8,128)S(1)}, f32[5,16,512]{2,1,0:T(8,128)S(1)}, u32[]{:S(2)}, u32[]{:S(2)}) %collective-permute-start.21) | collective-permute-done | bytes 163872 | tf_op jit(solution)/shard_map/ppermute | solution.py:1036
  183.1 2.1 collective-permute-start.25
  185.2 4.0 %collective-permute-done.25.new_ref = f32[1,16,1664]{2,1,0:T(8,128)S(1)} collective-permute-done((f32[1,16,1664]{2,1,0:T(8,128)S(1)}, f32[1,16,1664]{2,1,0:T(8,128)S(1)}, u32[]{:S(2)}, u32[]{:S(2)}) %collective-permute-start.25) | collective-permute-done | bytes 106528 | tf_op jit(solution)/shard_map/ppermute | solution.py:1036
  189.7 1.9 collective-permute-done.24.other_ref
  192.8 1.3 collective-permute-start.29
  194.1 1.5 collective-permute-start.26
  195.6 6.5 %shard_map.367 = (bf16[4,256,512]{2,1,0:T(8,128)(2,1)}, f32[8,128]{1,0:T(8,128)}) custom-call(s32[1]{0:T(128)} %bitcast.refs_0_, bf16[1024,2048]{1,0:T(8,128)(2,1)} %get-tuple-element.167.refs_1_, f32[4,256,512]{2,1,0:T(8,128)} %get-tuple-element.168.refs_4_.refs_2_, bf16[2048,512]{1,0:T(8,128)(2,1)} %refs_3_.5, f32[1,512]{1,0:T(1,128)} %bitcast.28, ...), custom_call_target="tpu_custom_call" | custom-call | flops 2147483648 | bytes 20000000 | tf_op jit(solution)/shard_map/pallas_call | solution.py:1238
  205.5 1.4 down_join1.1
  207.0 2.1 collective-permute-start.27
  209.0 6.1 %collective-permute-done.27.other_ref = f32[1,32,1664]{2,1,0:T(8,128)S(1)} collective-permute-done((f32[1,32,1664]{2,1,0:T(8,128)S(1)}, f32[1,32,1664]{2,1,0:T(8,128)S(1)}, u32[]{:S(2)}, u32[]{:S(2)}) %collective-permute-start.27) | collective-permute-done | bytes 213024 | tf_op jit(solution)/shard_map/ppermute | solution.py:1036
  215.7 1.3 collective-permute-start.30
  217.0 9.9 %collective-permute-done.31.other_ref = f32[5,128,512]{2,1,0:T(8,128)S(1)} collective-permute-done((f32[5,128,512]{2,1,0:T(8,128)S(1)}, f32[5,128,512]{2,1,0:T(8,128)S(1)}, u32[]{:S(2)}, u32[]{:S(2)}) %collective-permute-start.31) | collective-permute-done | bytes 1310752 | tf_op jit(solution)/shard_map/ppermute | solution.py:1036
  229.2 2.8 %down_place.1 = (f32[2048,512]{1,0:T(8,128)}, f32[8,128]{1,0:T(8,128)S(1)}) custom-call(s32[5]{0:T(128)S(1)} %copy-done.4, f32[1,1024,512]{2,1,0:T(8,128)S(1)} %get-tuple-element.271.own_ref, f32[1,1024,512]{2,1,0:T(8,128)S(1)} %collective-permute-done.33.other_ref, f32[8,128]{1,0:T(8,128)S(1)} %get-tuple-element.272.token_ref), custom_call_target="tpu_custom_call" | custom-call | bytes 40000000 | tf_op jit(solution)/shard_map/down_place/pallas_call | solution.py:1040
  232.0 9.1 %collective-permute-done.32.other_ref = f32[1,128,1664]{2,1,0:T(8,128)S(1)} collective-permute-done((f32[1,128,1664]{2,1,0:T(8,128)S(1)}, f32[1,128,1664]{2,1,0:T(8,128)S(1)}, u32[]{:S(2)}, u32[]{:S(2)}) %collective-permute-start.32) | collective-permute-done | bytes 852000 | tf_op jit(solution)/shard_map/ppermute | solution.py:1036
  241.9 3.2 %up_place.1 = (f32[512,2048]{1,0:T(8,128)}, f32[512,512]{1,0:T(8,128)}, f32[8,128]{1,0:T(8,128)S(1)}) custom-call(s32[5]{0:T(128)S(1)} %copy-done.4, f32[5,256,512]{2,1,0:T(8,128)S(1)} %get-tuple-element.275.own_ref, f32[5,256,512]{2,1,0:T(8,128)S(1)} %collective-permute-done.35.other_ref, f32[8,128]{1,0:T(8,128)S(1)} %get-tuple-element.276.token_ref), custom_call_target="tpu_custom_call" | custom-call | bytes 40000000 | tf_op jit(solution)/shard_map/up_place/pallas_call | solution.py:1040
  245.4 2.3 last_place.1
  (104 shorter events, 30.3 us)
Async XLA Ops:
  7.1 13.5 %collective-permute-start = (f32[4,16,1024]{2,1,0:T(8,128)}, f32[4,16,1024]{2,1,0:T(8,128)S(1)}, u32[]{:S(2)}, u32[]{:S(2)}) collective-permute-start(f32[4,16,1024]{2,1,0:T(8,128)} %get-tuple-element.162), channel_id=1, source_target_pairs={{0,8},{8,0},{16,24},{24,16},{1,9},{9,1},{17,25},{25,17},{2,10},{10... | collective-permute-start | bytes 786440 | tf_op jit(solution)/shard_map/ppermute | solution.py:1340
  10.1 10.5 %collective-permute-start.2 = (f32[4,8,1024]{2,1,0:T(8,128)}, f32[4,8,1024]{2,1,0:T(8,128)S(1)}, u32[]{:S(2)}, u32[]{:S(2)}) collective-permute-start(f32[4,8,1024]{2,1,0:T(8,128)} %get-tuple-element.163), channel_id=1, source_target_pairs={{0,24},{8,16},{16,8},{24,0},{1,25},{9,17},{17,9},{25,1},{2,26},{10... | collective-permute-start | bytes 393224 | tf_op jit(solution)/shard_map/ppermute | solution.py:1340
  11.6 9.0 %collective-permute-start.1 = (f32[4,8,1024]{2,1,0:T(8,128)}, f32[4,8,1024]{2,1,0:T(8,128)S(1)}, u32[]{:S(2)}, u32[]{:S(2)}) collective-permute-start(f32[4,8,1024]{2,1,0:T(8,128)} %get-tuple-element.163), channel_id=1, source_target_pairs={{0,16},{8,24},{16,0},{24,8},{1,17},{9,25},{17,1},{25,9},{2,18},{10... | collective-permute-start | bytes 393224 | tf_op jit(solution)/shard_map/ppermute | solution.py:1340
  20.6 0.7 copy-start.15
  20.6 0.8 copy-start.12
  49.2 15.5 %collective-permute-start.4 = (f32[1,1024,512]{2,1,0:T(8,128)}, f32[1,1024,512]{2,1,0:T(8,128)}, u32[]{:S(2)}, u32[]{:S(2)}) collective-permute-start(f32[1,1024,512]{2,1,0:T(8,128)} %get-tuple-element.185), channel_id=1, source_target_pairs={{0,1},{1,0},{2,3},{3,2},{4,5},{5,4},{6,7},{7,6},{8,9},{9,8},{10,11... | collective-permute-start | bytes 6291464 | tf_op jit(solution)/shard_map/ppermute | solution.py:1036
  60.1 15.9 %collective-permute-start.3 = (f32[5,256,512]{2,1,0:T(8,128)}, f32[5,256,512]{2,1,0:T(8,128)}, u32[]{:S(2)}, u32[]{:S(2)}) collective-permute-start(f32[5,256,512]{2,1,0:T(8,128)} %get-tuple-element.177), channel_id=1, source_target_pairs={{0,1},{1,0},{2,3},{3,2},{4,5},{5,4},{6,7},{7,6},{8,9},{9,8},{10,11... | collective-permute-start | bytes 7864328 | tf_op jit(solution)/shard_map/ppermute | solution.py:1036
  60.6 13.1 %collective-permute-start.5 = (f32[4,16,1024]{2,1,0:T(8,128)}, f32[4,16,1024]{2,1,0:T(8,128)S(1)}, u32[]{:S(2)}, u32[]{:S(2)}) collective-permute-start(f32[4,16,1024]{2,1,0:T(8,128)} %get-tuple-element.191), channel_id=1, source_target_pairs={{0,8},{8,0},{16,24},{24,16},{1,9},{9,1},{17,25},{25,17},{2,10},{10... | collective-permute-start | bytes 786440 | tf_op jit(solution)/shard_map/ppermute | solution.py:1340
  62.7 11.0 %collective-permute-start.6 = (f32[4,8,1024]{2,1,0:T(8,128)}, f32[4,8,1024]{2,1,0:T(8,128)S(1)}, u32[]{:S(2)}, u32[]{:S(2)}) collective-permute-start(f32[4,8,1024]{2,1,0:T(8,128)} %get-tuple-element.192), channel_id=1, source_target_pairs={{0,16},{8,24},{16,0},{24,8},{1,17},{9,25},{17,1},{25,9},{2,18},{10... | collective-permute-start | bytes 393224 | tf_op jit(solution)/shard_map/ppermute | solution.py:1340
  64.2 9.5 %collective-permute-start.7 = (f32[4,8,1024]{2,1,0:T(8,128)}, f32[4,8,1024]{2,1,0:T(8,128)S(1)}, u32[]{:S(2)}, u32[]{:S(2)}) collective-permute-start(f32[4,8,1024]{2,1,0:T(8,128)} %get-tuple-element.193), channel_id=1, source_target_pairs={{0,24},{8,16},{16,8},{24,0},{1,25},{9,17},{17,9},{25,1},{2,26},{10... | collective-permute-start | bytes 393224 | tf_op jit(solution)/shard_map/ppermute | solution.py:1340
  73.7 0.7 copy-start.18
  73.7 0.8 copy-start.16
  74.5 15.0 %collective-permute-start.9 = (f32[1,512,512]{2,1,0:T(8,128)}, f32[1,512,512]{2,1,0:T(8,128)S(1)}, u32[]{:S(2)}, u32[]{:S(2)}) collective-permute-start(f32[1,512,512]{2,1,0:T(8,128)} %get-tuple-element.198), channel_id=1, source_target_pairs={{0,8},{1,17},{2,10},{3,19},{4,12},{5,21},{6,14},{7,23},{8,0},{9,25... | collective-permute-start | bytes 3145736 | tf_op jit(solution)/shard_map/ppermute | solution.py:1036
  84.6 26.9 %collective-permute-start.8 = (f32[5,128,512]{2,1,0:T(8,128)}, f32[5,128,512]{2,1,0:T(8,128)}, u32[]{:S(2)}, u32[]{:S(2)}) collective-permute-start(f32[5,128,512]{2,1,0:T(8,128)} %get-tuple-element.197), channel_id=1, source_target_pairs={{0,8},{1,17},{2,10},{3,19},{4,12},{5,21},{6,14},{7,23},{8,0},{9,25... | collective-permute-start | bytes 3932168 | tf_op jit(solution)/shard_map/ppermute | solution.py:1036
  89.5 1.0 copy-start.13
  94.4 13.5 %collective-permute-start.10 = (f32[1,256,512]{2,1,0:T(8,128)}, f32[1,256,512]{2,1,0:T(8,128)S(1)}, u32[]{:S(2)}, u32[]{:S(2)}) collective-permute-start(f32[1,256,512]{2,1,0:T(8,128)} %get-tuple-element.201), channel_id=1, source_target_pairs={{0,16},{1,9},{2,18},{3,11},{4,20},{5,13},{6,22},{7,15},{8,24},{9,1... | collective-permute-start | bytes 1572872 | tf_op jit(solution)/shard_map/ppermute | solution.py:1036
  95.9 12.0 %copy-start.2 = (f32[1,256,512]{2,1,0:T(8,128)S(1)}, f32[1,256,512]{2,1,0:T(8,128)}, u32[]{:S(2)}) copy-start(f32[1,256,512]{2,1,0:T(8,128)} %get-tuple-element.200.keep_ref) | copy-start | bytes 1572868
  95.9 12.0 %copy-start.3 = (s32[5]{0:T(128)S(1)}, s32[5]{0:T(128)}, u32[]{:S(2)}) copy-start(s32[5]{0:T(128)} %stack.31.refs_2_.bits_ref) | copy-start | bytes 64
  108.0 0.7 copy-start.5
  109.8 7.6 %collective-permute-start.12 = (f32[1,128,512]{2,1,0:T(8,128)S(1)}, f32[1,128,512]{2,1,0:T(8,128)S(1)}, u32[]{:S(2)}, u32[]{:S(2)}) collective-permute-start(f32[1,128,512]{2,1,0:T(8,128)S(1)} %get-tuple-element.219), channel_id=1, source_target_pairs={{0,2},{1,5},{2,0},{3,7},{4,6},{5,1},{6,4},{7,3},{8,10},{9,13},{10,... | collective-permute-start | bytes 786440 | tf_op jit(solution)/shard_map/ppermute | solution.py:1036
  111.4 6.0 %copy-start.4 = (s32[5]{0:T(128)S(1)}, s32[5]{0:T(128)}, u32[]{:S(2)}) copy-start(s32[5]{0:T(128)} %stack.31.refs_2_.bits_ref) | copy-start | bytes 64
  115.7 12.8 %copy-start = (f32[1,256,1664]{2,1,0:T(8,128)S(1)}, f32[1,256,1664]{2,1,0:T(8,128)}, u32[]{:S(2)}) copy-start(f32[1,256,1664]{2,1,0:T(8,128)} %get-tuple-element.216.keep_ref) | copy-start | bytes 5111812
  119.3 11.7 %copy-start.1 = (f32[5,64,512]{2,1,0:T(8,128)S(1)}, f32[5,64,512]{2,1,0:T(8,128)}, u32[]{:S(2)}) copy-start(f32[5,64,512]{2,1,0:T(8,128)} %get-tuple-element.214.keep_ref) | copy-start | bytes 1966084
  119.3 9.3 %collective-permute-start.13 = (f32[1,256,1664]{2,1,0:T(8,128)}, f32[1,256,1664]{2,1,0:T(8,128)S(1)}, u32[]{:S(2)}, u32[]{:S(2)}) collective-permute-start(f32[1,256,1664]{2,1,0:T(8,128)} %get-tuple-element.222), channel_id=1, source_target_pairs={{0,1},{1,0},{2,3},{3,2},{4,5},{5,4},{6,7},{7,6},{8,9},{9,8},{10,11... | collective-permute-start | bytes 5111816 | tf_op jit(solution)/shard_map/ppermute | solution.py:1036
  119.9 11.1 %collective-permute-start.11 = (f32[5,64,512]{2,1,0:T(8,128)}, f32[5,64,512]{2,1,0:T(8,128)S(1)}, u32[]{:S(2)}, u32[]{:S(2)}) collective-permute-start(f32[5,64,512]{2,1,0:T(8,128)} %get-tuple-element.215), channel_id=1, source_target_pairs={{0,16},{1,9},{2,18},{3,11},{4,20},{5,13},{6,22},{7,15},{8,24},{9,1... | collective-permute-start | bytes 1966088 | tf_op jit(solution)/shard_map/ppermute | solution.py:1036
  121.4 6.0 %collective-permute-start.14 = (f32[1,64,512]{2,1,0:T(8,128)S(1)}, f32[1,64,512]{2,1,0:T(8,128)S(1)}, u32[]{:S(2)}, u32[]{:S(2)}) collective-permute-start(f32[1,64,512]{2,1,0:T(8,128)S(1)} %get-tuple-element.224), channel_id=1, source_target_pairs={{0,4},{1,3},{2,6},{3,1},{4,0},{5,7},{6,2},{7,5},{8,12},{9,11},{10,... | collective-permute-start | bytes 393224 | tf_op jit(solution)/shard_map/ppermute | solution.py:1036
  129.4 16.4 %collective-permute-start.19 = (f32[1,128,1664]{2,1,0:T(8,128)S(1)}, f32[1,128,1664]{2,1,0:T(8,128)S(1)}, u32[]{:S(2)}, u32[]{:S(2)}) collective-permute-start(f32[1,128,1664]{2,1,0:T(8,128)S(1)} %get-tuple-element.236), channel_id=1, source_target_pairs={{0,8},{1,17},{2,10},{3,19},{4,12},{5,21},{6,14},{7,23},{8,0},{9,25... | collective-permute-start | bytes 2555912 | tf_op jit(solution)/shard_map/ppermute | solution.py:1036
  131.6 13.1 %collective-permute-start.15 = (f32[5,32,512]{2,1,0:T(8,128)S(1)}, f32[5,32,512]{2,1,0:T(8,128)S(1)}, u32[]{:S(2)}, u32[]{:S(2)}) collective-permute-start(f32[5,32,512]{2,1,0:T(8,128)S(1)} %get-tuple-element.229), channel_id=1, source_target_pairs={{0,2},{1,5},{2,0},{3,7},{4,6},{5,1},{6,4},{7,3},{8,10},{9,13},{10,... | collective-permute-start | bytes 983048 | tf_op jit(solution)/shard_map/ppermute | solution.py:1036
  133.7 11.6 %collective-permute-start.17 = (f32[1,64,512]{2,1,0:T(8,128)S(1)}, f32[1,64,512]{2,1,0:T(8,128)S(1)}, u32[]{:S(2)}, u32[]{:S(2)}) collective-permute-start(f32[1,64,512]{2,1,0:T(8,128)S(1)} %get-tuple-element.233.own_ref), channel_id=1, source_target_pairs={{0,4},{1,3},{2,6},{3,1},{4,0},{5,7},{6,2},{7,5},{8,12},{9,11},{10,... | collective-permute-start | bytes 393224 | tf_op jit(solution)/shard_map/ppermute | solution.py:1036
  146.7 8.2 %collective-permute-start.20 = (f32[1,64,1664]{2,1,0:T(8,128)S(1)}, f32[1,64,1664]{2,1,0:T(8,128)S(1)}, u32[]{:S(2)}, u32[]{:S(2)}) collective-permute-start(f32[1,64,1664]{2,1,0:T(8,128)S(1)} %get-tuple-element.239), channel_id=1, source_target_pairs={{0,16},{1,9},{2,18},{3,11},{4,20},{5,13},{6,22},{7,15},{8,24},{9,1... | collective-permute-start | bytes 1277960 | tf_op jit(solution)/shard_map/ppermute | solution.py:1036
  147.8 8.2 %collective-permute-start.18 = (f32[1,128,512]{2,1,0:T(8,128)S(1)}, f32[1,128,512]{2,1,0:T(8,128)S(1)}, u32[]{:S(2)}, u32[]{:S(2)}) collective-permute-start(f32[1,128,512]{2,1,0:T(8,128)S(1)} %get-tuple-element.235.own_ref), channel_id=1, source_target_pairs={{0,2},{1,5},{2,0},{3,7},{4,6},{5,1},{6,4},{7,3},{8,10},{9,13},{10,... | collective-permute-start | bytes 786440 | tf_op jit(solution)/shard_map/ppermute | solution.py:1036
  156.6 13.2 %collective-permute-start.22 = (f32[1,256,512]{2,1,0:T(8,128)S(1)}, f32[1,256,512]{2,1,0:T(8,128)S(1)}, u32[]{:S(2)}, u32[]{:S(2)}) collective-permute-start(f32[1,256,512]{2,1,0:T(8,128)S(1)} %get-tuple-element.244.own_ref), channel_id=1, source_target_pairs={{0,16},{1,9},{2,18},{3,11},{4,20},{5,13},{6,22},{7,15},{8,24},{9,1... | collective-permute-start | bytes 1572872 | tf_op jit(solution)/shard_map/ppermute | solution.py:1036
  158.1 10.3 %collective-permute-start.16 = (f32[5,16,512]{2,1,0:T(8,128)S(1)}, f32[5,16,512]{2,1,0:T(8,128)S(1)}, u32[]{:S(2)}, u32[]{:S(2)}) collective-permute-start(f32[5,16,512]{2,1,0:T(8,128)S(1)} %get-tuple-element.232), channel_id=1, source_target_pairs={{0,4},{1,3},{2,6},{3,1},{4,0},{5,7},{6,2},{7,5},{8,12},{9,11},{10,... | collective-permute-start | bytes 491528 | tf_op jit(solution)/shard_map/ppermute | solution.py:1036
  159.9 9.3 %collective-permute-start.23 = (f32[1,32,1664]{2,1,0:T(8,128)S(1)}, f32[1,32,1664]{2,1,0:T(8,128)S(1)}, u32[]{:S(2)}, u32[]{:S(2)}) collective-permute-start(f32[1,32,1664]{2,1,0:T(8,128)S(1)} %get-tuple-element.246), channel_id=1, source_target_pairs={{0,2},{1,5},{2,0},{3,7},{4,6},{5,1},{6,4},{7,3},{8,10},{9,13},{10,... | collective-permute-start | bytes 638984 | tf_op jit(solution)/shard_map/ppermute | solution.py:1036
  169.0 12.7 %collective-permute-start.21 = (f32[5,16,512]{2,1,0:T(8,128)S(1)}, f32[5,16,512]{2,1,0:T(8,128)S(1)}, u32[]{:S(2)}, u32[]{:S(2)}) collective-permute-start(f32[5,16,512]{2,1,0:T(8,128)S(1)} %get-tuple-element.243.own_ref), channel_id=1, source_target_pairs={{0,4},{1,3},{2,6},{3,1},{4,0},{5,7},{6,2},{7,5},{8,12},{9,11},{10,... | collective-permute-start | bytes 491528 | tf_op jit(solution)/shard_map/ppermute | solution.py:1036
  182.2 9.4 %collective-permute-start.24 = (f32[5,32,512]{2,1,0:T(8,128)S(1)}, f32[5,32,512]{2,1,0:T(8,128)S(1)}, u32[]{:S(2)}, u32[]{:S(2)}) collective-permute-start(f32[5,32,512]{2,1,0:T(8,128)S(1)} %get-tuple-element.250.own_ref), channel_id=1, source_target_pairs={{0,2},{1,5},{2,0},{3,7},{4,6},{5,1},{6,4},{7,3},{8,10},{9,13},{10,... | collective-permute-start | bytes 983048 | tf_op jit(solution)/shard_map/ppermute | solution.py:1036
  182.3 23.2 %collective-permute-start.28 = (f32[1,512,512]{2,1,0:T(8,128)S(1)}, f32[1,512,512]{2,1,0:T(8,128)}, u32[]{:S(2)}, u32[]{:S(2)}) collective-permute-start(f32[1,512,512]{2,1,0:T(8,128)S(1)} %get-tuple-element.261.own_ref), channel_id=1, source_target_pairs={{0,8},{1,17},{2,10},{3,19},{4,12},{5,21},{6,14},{7,23},{8,0},{9,25... | collective-permute-start | bytes 3145736 | tf_op jit(solution)/shard_map/ppermute | solution.py:1036
  183.1 6.1 %collective-permute-start.25 = (f32[1,16,1664]{2,1,0:T(8,128)S(1)}, f32[1,16,1664]{2,1,0:T(8,128)S(1)}, u32[]{:S(2)}, u32[]{:S(2)}) collective-permute-start(f32[1,16,1664]{2,1,0:T(8,128)S(1)} %get-tuple-element.252), channel_id=1, source_target_pairs={{0,4},{1,3},{2,6},{3,1},{4,0},{5,7},{6,2},{7,5},{8,12},{9,11},{10,... | collective-permute-start | bytes 319496 | tf_op jit(solution)/shard_map/ppermute | solution.py:1036
  192.8 10.7 %collective-permute-start.29 = (f32[5,64,512]{2,1,0:T(8,128)S(1)}, f32[5,64,512]{2,1,0:T(8,128)}, u32[]{:S(2)}, u32[]{:S(2)}) collective-permute-start(f32[5,64,512]{2,1,0:T(8,128)S(1)} %get-tuple-element.262.own_ref), channel_id=1, source_target_pairs={{0,16},{1,9},{2,18},{3,11},{4,20},{5,13},{6,22},{7,15},{8,24},{9,1... | collective-permute-start | bytes 1966088 | tf_op jit(solution)/shard_map/ppermute | solution.py:1036
  194.1 8.0 %collective-permute-start.26 = (f32[1,16,1664]{2,1,0:T(8,128)S(1)}, f32[1,16,1664]{2,1,0:T(8,128)S(1)}, u32[]{:S(2)}, u32[]{:S(2)}) collective-permute-start(f32[1,16,1664]{2,1,0:T(8,128)S(1)} %get-tuple-element.258.own_ref), channel_id=1, source_target_pairs={{0,4},{1,3},{2,6},{3,1},{4,0},{5,7},{6,2},{7,5},{8,12},{9,11},{10,... | collective-permute-start | bytes 319496 | tf_op jit(solution)/shard_map/ppermute | solution.py:1036
  202.1 0.7 copy-start.11
  204.7 22.2 %collective-permute-start.31 = (f32[5,128,512]{2,1,0:T(8,128)S(1)}, f32[5,128,512]{2,1,0:T(8,128)S(1)}, u32[]{:S(2)}, u32[]{:S(2)}) collective-permute-start(f32[5,128,512]{2,1,0:T(8,128)S(1)} %get-tuple-element.267.own_ref), channel_id=1, source_target_pairs={{0,8},{1,17},{2,10},{3,19},{4,12},{5,21},{6,14},{7,23},{8,0},{9,25... | collective-permute-start | bytes 3932168 | tf_op jit(solution)/shard_map/ppermute | solution.py:1036
  206.9 22.3 %collective-permute-start.33 = (f32[1,1024,512]{2,1,0:T(8,128)S(1)}, f32[1,1024,512]{2,1,0:T(8,128)S(1)}, u32[]{:S(2)}, u32[]{:S(2)}) collective-permute-start(f32[1,1024,512]{2,1,0:T(8,128)S(1)} %get-tuple-element.271.own_ref), channel_id=1, source_target_pairs={{0,1},{1,0},{2,3},{3,2},{4,5},{5,4},{6,7},{7,6},{8,9},{9,8},{10,11... | collective-permute-start | bytes 6291464 | tf_op jit(solution)/shard_map/ppermute | solution.py:1036
  207.0 8.2 %collective-permute-start.27 = (f32[1,32,1664]{2,1,0:T(8,128)S(1)}, f32[1,32,1664]{2,1,0:T(8,128)S(1)}, u32[]{:S(2)}, u32[]{:S(2)}) collective-permute-start(f32[1,32,1664]{2,1,0:T(8,128)S(1)} %get-tuple-element.260.own_ref), channel_id=1, source_target_pairs={{0,2},{1,5},{2,0},{3,7},{4,6},{5,1},{6,4},{7,3},{8,10},{9,13},{10,... | collective-permute-start | bytes 638984 | tf_op jit(solution)/shard_map/ppermute | solution.py:1036
  215.7 12.0 %collective-permute-start.30 = (f32[1,64,1664]{2,1,0:T(8,128)S(1)}, f32[1,64,1664]{2,1,0:T(8,128)S(1)}, u32[]{:S(2)}, u32[]{:S(2)}) collective-permute-start(f32[1,64,1664]{2,1,0:T(8,128)S(1)} %get-tuple-element.266.own_ref), channel_id=1, source_target_pairs={{0,16},{1,9},{2,18},{3,11},{4,20},{5,13},{6,22},{7,15},{8,24},{9,1... | collective-permute-start | bytes 1277960 | tf_op jit(solution)/shard_map/ppermute | solution.py:1036
  227.6 14.2 %collective-permute-start.35 = (f32[5,256,512]{2,1,0:T(8,128)S(1)}, f32[5,256,512]{2,1,0:T(8,128)S(1)}, u32[]{:S(2)}, u32[]{:S(2)}) collective-permute-start(f32[5,256,512]{2,1,0:T(8,128)S(1)} %get-tuple-element.275.own_ref), channel_id=1, source_target_pairs={{0,1},{1,0},{2,3},{3,2},{4,5},{5,4},{6,7},{7,6},{8,9},{9,8},{10,11... | collective-permute-start | bytes 7864328 | tf_op jit(solution)/shard_map/ppermute | solution.py:1036
  228.3 12.8 %collective-permute-start.32 = (f32[1,128,1664]{2,1,0:T(8,128)S(1)}, f32[1,128,1664]{2,1,0:T(8,128)S(1)}, u32[]{:S(2)}, u32[]{:S(2)}) collective-permute-start(f32[1,128,1664]{2,1,0:T(8,128)S(1)} %get-tuple-element.270.own_ref), channel_id=1, source_target_pairs={{0,8},{1,17},{2,10},{3,19},{4,12},{5,21},{6,14},{7,23},{8,0},{9,25... | collective-permute-start | bytes 2555912 | tf_op jit(solution)/shard_map/ppermute | solution.py:1036
  241.8 3.7 %collective-permute-start.34 = (f32[1,256,1664]{2,1,0:T(8,128)S(1)}, f32[1,256,1664]{2,1,0:T(8,128)S(1)}, u32[]{:S(2)}, u32[]{:S(2)}) collective-permute-start(f32[1,256,1664]{2,1,0:T(8,128)S(1)} %get-tuple-element.274.own_ref), channel_id=1, source_target_pairs={{0,1},{1,0},{2,3},{3,2},{4,5},{5,4},{6,7},{7,6},{8,9},{9,8},{10,11... | collective-permute-start | bytes 5111816 | tf_op jit(solution)/shard_map/ppermute | solution.py:1036
  (7 other events, 4.5 us)

commit v2 on v1

--- a/solution.py
+++ b/solution.py
@@ -20,7 +20,7 @@
 MASKED = -1e30
 TOKEN = (8, 128)
 ROUND_BYTES = dict(down=40_000_000, up=40_000_000, last=40_000_000)
-ROUNDS = "u,d,ud,dudldluudlldulduluoludluldlul"
+ROUNDS = "u,d,ud,dudldluudlluddlululudlouldlul"
 TILE = 32
 EPSILON = 1e-05
 VMEM_BYTES = 62 * 2**20
@@ -250,7 +250,7 @@
     queries_wide = dot(normed, query_weight_ref[...])
     value_bias, query_bias = value_bias_ref[...], query_bias_ref[...]
     for at in range(count):
-        remaining = lengths_ref[pl.program_id(0) * count + at] - shard_ref[0] * tok_count
+        remaining = lengths_ref[pl.program_id(0) * count + at] - shard_ref[shard_ref.shape[0] - 1] * tok_count
         for rows in tiles(tok_count):
             places = slice(at * tok_count + rows.start, at * tok_count + rows.stop)
             valid = iota((TILE, width), 0) + rows.start < remaining
@@ -286,7 +286,7 @@
 ):
     sequence = pl.program_id(0)
     tok_count = keys_ref.shape[1]
-    remaining = lengths_ref[sequence] - shard_ref[0] * tok_count
+    remaining = lengths_ref[sequence] - shard_ref[shard_ref.shape[0] - 1] * tok_count
     inverse = coarse_inverse(remaining)
     pooled_keys_ref[0] = pooled_keys(members_ref[...], keys_ref[0], inverse)
     pooled_values_ref[0] = pooled_keys(members_ref[...], values_ref[0], inverse)
@@ -425,7 +425,7 @@
 
     def work(own):
         far_keys, far_values, far_bias, _ = far_state(
-            pl.program_id(0) * count + own, lengths_ref, shard_ref[0], tok_count, heights, shards, pieces
+            pl.program_id(0) * count + own, lengths_ref, shard_ref[shard_ref.shape[0] - 1], tok_count, heights, shards, pieces
         )
         coarse = far_queries_of(queries_ref[own], spread_ref, heights)
         for at in range(heights):
@@ -610,7 +610,7 @@
 
     def work(own):
         far_keys, far_values, far_bias, inverse = far_state(
-            step * count + own, lengths_ref, shard_ref[0], tok_count, heights, shards, pieces
+            step * count + own, lengths_ref, shard_ref[shard_ref.shape[0] - 1], tok_count, heights, shards, pieces
         )
         coarse = [far_ref[own, :, at * tok_count : (at + 1) * tok_count] for at in range(heights)]
         logits = [dot(far_keys[at], coarse[at]) for at in range(heights)]
@@ -687,7 +687,7 @@
 
     @pl.when(step == pl.num_programs(0) - 1)
     def _():
-        split_rows(weights_ref, shard_ref[1], send_ref.at[0], keep_ref.at[0])
+        split_rows(weights_ref, shard_ref[0], send_ref.at[0], keep_ref.at[0])
 
 
 def near_back_kernel(
@@ -716,7 +716,7 @@
         send_ref[...] = keep_ref[...] + other_ref[...]
     sequence = pl.program_id(0) + begin
     tok_count = keys_ref.shape[1]
-    remaining = lengths_ref[sequence] - shard_ref[0] * tok_count
+    remaining = lengths_ref[sequence] - shard_ref[shard_ref.shape[0] - 1] * tok_count
     inverse = coarse_inverse(remaining)
     keys = chunk_keys(keys_ref[0], pooled_keys_ref[0])
     values = chunk_keys(values_ref[0], pooled_values_ref[0])
@@ -843,7 +843,7 @@
 
     gain, shift = gain_ref[...], shift_ref[...]
     for at in range(count):
-        remaining = lengths_ref[sequence * count + at] - shard_ref[0] * tok_count
+        remaining = lengths_ref[sequence * count + at] - shard_ref[shard_ref.shape[0] - 1] * tok_count
         far = [
             sum(piece[at] for piece, level in zip(pieces, piece_heights) if level == height)
             for height in range(heights)
@@ -896,7 +896,7 @@
                 weights_ref[at : at + 1, 3 * width :] = small_ref[
                     line : line + 1, part * CHUNK : (part + 1) * CHUNK
                 ]
-        split_rows(weights_ref, shard_ref[1], send_ref.at[0], keep_ref.at[0])
+        split_rows(weights_ref, shard_ref[0], send_ref.at[0], keep_ref.at[0])
 
 
 def half_of(ref, bit):
@@ -1022,8 +1022,8 @@
             bits.append(jnp.where(core == 0, one, other))
         self.steps = len(bits)
         self.token = None
-        self.bits = jnp.stack(bits).astype(jnp.int32)
-        self.pairs = [[] for _ in bits]
+        self.bits = jnp.stack(bits + [places["seq"]]).astype(jnp.int32)
+        self.pairs = [[] for _ in range(self.steps)]
         for seq in range(self.shards):
             for batch in range(self.batches):
                 moves = [("batch", 0)] + orders[batch & 1]
@@ -1279,12 +1279,10 @@
     seq_count, tok_count, width = tokens.shape
     inner_width = up_weight.shape[1]
     shards = lax.axis_size("seq")
-    shard_index = lax.axis_index("seq")
     heights = shards.bit_length() - 1
     grid = (seq_count,)
     reducer = Reducer()
-    core = reducer.bits[:1]
-    shard = jnp.stack([shard_index.astype(jnp.int32), reducer.bits[0]])
+    core = shard = reducer.bits
 
     def row(vector):
         return vector.reshape(1, -1)

time: 249 us -> 240 us (0.964)
  waiting for transfers between devices: 73.1 us -> 58.9 us
  Pallas kernels: 121 us -> 126 us
    ppermute x30, waiting for transfers between devices: 72.5 us -> 58.3 us  [swap(): return lax.ppermute(array, ('seq', 'batch'), self.pairs[step])]
    pallas_call x28, Pallas kernels: 32 us -> 35.1 us  [run(): pl.pallas_call(kernel, in_specs=[pl.BlockSpec(memory_space=pltpu.SMEM)] +...]
    unnamed x38 -> x40, local copies, waits for them, and re-layouts: 7.04 us -> 6.97 us
  transfers between devices with their start and end apart: 36 -> 36, of which waited for: 17 -> 18; matrix products, arithmetic and copies ran while one was open for 0% -> 0% of each run, Pallas kernels for 33% -> 36%
where the time goes in v2:
time: 240 us; the launch traced here: 239 us
  Pallas kernels  126 us (52%)
  waiting for transfers between devices  58.9 us (25%)
  starting transfers between devices  46.1 us (19%)
  local copies, waits for them, and re-layouts  7.57 us (3%)
    pallas_call x9, Pallas kernels, call(): pl.pallas_call(body, grid_spec=pltpu.PrefetchScalarGridSpec(num_scalar_pr...  90.5 us
    ppermute x30, waiting for transfers between devices, swap(): return lax.ppermute(array, ('seq', 'batch'), self.pairs[step])  58.3 us
    ppermute x30, starting transfers between devices, swap(): return lax.ppermute(array, ('seq', 'batch'), self.pairs[step])  38.1 us
    pallas_call x28, Pallas kernels, run(): pl.pallas_call(kernel, in_specs=[pl.BlockSpec(memory_space=pltpu.SMEM)] +...  35.1 us
    ppermute x6, starting transfers between devices, swap(): return lax.ppermute(array, 'seq', [(at, at ^ mask) for at in range(shards)])  8.01 us
    unnamed x40, local copies, waits for them, and re-layouts  6.97 us
  transfers between devices with their start and end apart: 36, of which 18 were waited for; matrix products, arithmetic and copies ran while one was open for 0% of the time, Pallas kernels for 36%

profile of v2, /device:TPU:0, one launch (start us, length us, event | category | flops | bytes accessed | tf_op | source)
XLA Modules:
  0.0 239.3 jit_solution(1465234637051656458)
XLA Ops:
  1.3 5.9 %shard_map.359 = (bf16[4,512,256]{2,1,0:T(8,128)(2,1)}, bf16[4,256,512]{2,1,0:T(8,128)(2,1)}, bf16[4,256,512]{2,1,0:T(8,128)(2,1)}, f32[4,16,1024]{2,1,0:T(8,128...) custom-call(s32[4]{0:T(128)} %refs_0_.13, s32[6]{0:T(128)} %stack.27.refs_1_.refs_0_.refs_2_.bits_ref, ...), custom_call_target="tpu_custom_call" | custom-call | flops 1610612736 | bytes 20000000 | tf_op jit(solution)/shard_map/pallas_call | solution.py:1238
  7.2 3.0 %collective-permute-start = (f32[4,16,1024]{2,1,0:T(8,128)}, f32[4,16,1024]{2,1,0:T(8,128)S(1)}, u32[]{:S(2)}, u32[]{:S(2)}) collective-permute-start(f32[4,16,1024]{2,1,0:T(8,128)} %get-tuple-element.162), channel_id=1, source_target_pairs={{0,8},{8,0},{16,24},{24,16},{1,9},{9,1},{17,25},{25,17},{2,10},{10... | collective-permute-start | bytes 786440 | tf_op jit(solution)/shard_map/ppermute | solution.py:1338
  10.1 1.5 collective-permute-start.2
  11.7 8.5 %shard_map.360 = (f32[4,8,256]{2,1,0:T(8,128)}, f32[4,8,256]{2,1,0:T(8,128)}, bf16[4,512,256]{2,1,0:T(8,128)(2,1)}, bf16[4,512,768]{2,1,0:T(8,128)(2,1)}, bf16[4...) custom-call(s32[4]{0:T(128)} %refs_0_.13, s32[6]{0:T(128)} %stack.27.refs_1_.refs_0_.refs_2_.bits_ref, ...), custom_call_target="tpu_custom_call" | custom-call | flops 1000000000 | bytes 20000000 | tf_op jit(solution)/shard_map/pallas_call | solution.py:1238
  21.5 7.6 %shard_map.361 = (f32[4,256,512]{2,1,0:T(8,128)}, bf16[4,256,512]{2,1,0:T(8,128)(2,1)}, f32[4,512,256]{2,1,0:T(8,128)}, f32[4,8,256]{2,1,0:T(8,128)}, bf16[4,512,512]{2,1,0:T(8,128)(2,1)}, /*index=5*/f32[8,128]{1,0:T(8,128)}) custom-call(s32[4]{0:T(128)} %refs_0_.13, s32[6]{0:T(128)} %stack.27.refs_1_.refs_0_.refs_2_.bits_ref, bf16[4,256,512]{2,1,0:T(8,128)(2,1)} %refs_2_.9, ...), custom_call_target="tpu_custom_call" | custom-call | flops 536870912 | bytes 20000000 | tf_op jit(solution)/shard_map/pallas_call | solution.py:1238
  29.1 20.9 %shard_map.362 = (bf16[4,256,512]{2,1,0:T(8,128)(2,1)}, f32[1,1024,512]{2,1,0:T(8,128)}, f32[1,1024,512]{2,1,0:T(8,128)}, f32[5,256,512]{2,1,0:T(8,128)}, f32[5,...) custom-call(s32[6]{0:T(128)} %stack.27.refs_1_.refs_0_.refs_2_.bits_ref, ...), custom_call_target="tpu_custom_call" | custom-call | flops 10737418240 | bytes 20000000 | tf_op jit(solution)/shard_map/pallas_call | solution.py:1238
  49.9 10.8 %shard_map.363 = (f32[4,256,512]{2,1,0:T(8,128)}, bf16[4,512,256]{2,1,0:T(8,128)(2,1)}, f32[4,8,256]{2,1,0:T(8,128)}, bf16[4,512,256]{2,1,0:T(8,128)(2,1)}, f32[...) custom-call(s32[4]{0:T(128)} %refs_0_.13, ...), custom_call_target="tpu_custom_call", output_to_operand_aliasing={{7}: (14, {}), {8}: (15, {})} | custom-call | flops 1073741824 | bytes 20000000 | tf_op jit(solution)/shard_map/pallas_call | solution.py:1238
  61.3 1.5 collective-permute-start.5
  62.8 1.5 collective-permute-start.6
  64.8 9.0 %shard_map.364 = (bf16[4,512,256]{2,1,0:T(8,128)(2,1)}, f32[4,256,512]{2,1,0:T(8,128)}, bf16[4,256,512]{2,1,0:T(8,128)(2,1)}, f32[1,512,512]{2,1,0:T(8,128)}, f32[8,128]{1,0:T(8,128)}) custom-call(s32[4]{0:T(128)} %refs_0_.13, s32[6]{0:T(128)} %stack.27.refs_1_.refs_0_.refs_2_.bits_ref, s32[6]{0:T(128)} %stack.27.refs_1_.refs_0_.refs_2_.bits_ref, ...), custom_call_target="tpu_custom_call" | custom-call | flops 2000000000 | bytes 20000000 | tf_op jit(solution)/shard_map/pallas_call | solution.py:1238
  74.6 1.5 collective-permute-start.8
  76.1 8.6 %shard_map.365 = (bf16[4,512,256]{2,1,0:T(8,128)(2,1)}, f32[4,256,512]{2,1,0:T(8,128)}, bf16[4,256,512]{2,1,0:T(8,128)(2,1)}, f32[5,128,512]{2,1,0:T(8,128)}, f32[8,128]{1,0:T(8,128)}) custom-call(s32[4]{0:T(128)} %refs_0_.13, s32[6]{0:T(128)} %stack.27.refs_1_.refs_0_.refs_2_.bits_ref, ...), custom_call_target="tpu_custom_call", output_to_operand_aliasing={{0}: (15, {}), {1}: (16, {}), {2}: (17, {})} | custom-call | flops 2000000000 | bytes 20000000 | tf_op jit(solution)/shard_map/pallas_call | solution.py:1238
  85.3 4.3 %collective-permute-done.8.new_ref = f32[1,512,512]{2,1,0:T(8,128)S(1)} collective-permute-done((f32[1,512,512]{2,1,0:T(8,128)}, f32[1,512,512]{2,1,0:T(8,128)S(1)}, u32[]{:S(2)}, u32[]{:S(2)}) %collective-permute-start.8) | collective-permute-done | bytes 1048608 | tf_op jit(solution)/shard_map/ppermute | solution.py:1036
  90.6 3.9 %down_sum2.1 = (f32[1,256,512]{2,1,0:T(8,128)}, f32[1,256,512]{2,1,0:T(8,128)}, f32[8,128]{1,0:T(8,128)}) custom-call(s32[6]{0:T(128)} %stack.27.refs_1_.refs_0_.refs_2_.bits_ref, f32[1,1024,512]{2,1,0:T(8,128)} %get-tuple-element.183.refs_15_.keep_ref, f32[1,1024,512]{2,1,0:T(8,128)} %collective-permute-done.3.refs_16_.other_ref, ...), custom_call_target="tpu_custom_call" | custom-call | bytes 40000000 | tf_op jit(solution)/shard_map/down_sum2/pallas_call | solution.py:1040
  94.5 1.5 collective-permute-start.9
  96.0 12.0 %shard_map.366 = (f32[4,256,512]{2,1,0:T(8,128)}, f32[1,256,1664]{2,1,0:T(8,128)}, f32[1,256,1664]{2,1,0:T(8,128)}, f32[8,128]{1,0:T(8,128)}) custom-call(s32[4]{0:T(128)} %refs_0_.13, s32[6]{0:T(128)} %stack.27.refs_1_.refs_0_.refs_2_.bits_ref, bf16[4,256,512]{2,1,0:T(8,128)(2,1)} %refs_2_.9, f32[4,256,512]{2,1,0:T(8,128)} %get-tuple-element.176.refs_3_, ...), custom_call_target="tpu_custom_call" | custom-call | flops 3221225472 | bytes 20000000 | tf_op jit(solution)/shard_map/pallas_call | solution.py:1238
  110.0 1.6 collective-permute-start.10
  111.5 4.3 %up_sum2.1 = (f32[5,64,512]{2,1,0:T(8,128)}, f32[5,64,512]{2,1,0:T(8,128)}, f32[8,128]{1,0:T(8,128)}) custom-call(s32[6]{0:T(128)} %stack.27.refs_1_.refs_0_.refs_2_.bits_ref, f32[5,256,512]{2,1,0:T(8,128)} %get-tuple-element.189.refs_18_.keep_ref, f32[5,256,512]{2,1,0:T(8,128)} %collective-permute-done.4.refs_19_.other_ref, ...), custom_call_target="tpu_custom_call" | custom-call | bytes 40000000 | tf_op jit(solution)/shard_map/up_sum2/pallas_call | solution.py:1040
  115.9 1.7 collective-permute-done.10.new_ref
  120.0 1.5 collective-permute-start.16
  121.5 2.4 collective-permute-start.13
  123.8 3.6 %collective-permute-done.13.new_ref = f32[1,64,512]{2,1,0:T(8,128)S(1)} collective-permute-done((f32[1,64,512]{2,1,0:T(8,128)S(1)}, f32[1,64,512]{2,1,0:T(8,128)S(1)}, u32[]{:S(2)}, u32[]{:S(2)}) %collective-permute-start.13) | collective-permute-done | bytes 131104 | tf_op jit(solution)/shard_map/ppermute | solution.py:1036
  129.5 1.5 collective-permute-start.14
  131.7 2.1 collective-permute-start.17
  133.8 3.1 %collective-permute-start.15 = (f32[1,64,512]{2,1,0:T(8,128)S(1)}, f32[1,64,512]{2,1,0:T(8,128)S(1)}, u32[]{:S(2)}, u32[]{:S(2)}) collective-permute-start(f32[1,64,512]{2,1,0:T(8,128)S(1)} %get-tuple-element.226.own_ref), channel_id=1, source_target_pairs={{0,4},{1,3},{2,6},{3,1},{4,0},{5,7},{6,2},{7,5},{8,12},{9,11},{10,... | collective-permute-start | bytes 393224 | tf_op jit(solution)/shard_map/ppermute | solution.py:1036
  136.9 7.9 %collective-permute-done.17.new_ref = f32[5,32,512]{2,1,0:T(8,128)S(1)} collective-permute-done((f32[5,32,512]{2,1,0:T(8,128)S(1)}, f32[5,32,512]{2,1,0:T(8,128)S(1)}, u32[]{:S(2)}, u32[]{:S(2)}) %collective-permute-start.17) | collective-permute-done | bytes 327712 | tf_op jit(solution)/shard_map/ppermute | solution.py:1036
  147.9 1.5 collective-permute-start.20
  149.4 2.4 collective-permute-start.21
  151.8 3.2 %collective-permute-done.18.new_ref = f32[1,64,1664]{2,1,0:T(8,128)S(1)} collective-permute-done((f32[1,64,1664]{2,1,0:T(8,128)S(1)}, f32[1,64,1664]{2,1,0:T(8,128)S(1)}, u32[]{:S(2)}, u32[]{:S(2)}) %collective-permute-start.18) | collective-permute-done | bytes 426016 | tf_op jit(solution)/shard_map/ppermute | solution.py:1036
  155.7 1.6 collective-permute-done.21.new_ref
  159.7 1.5 collective-permute-start.22
  162.6 1.7 collective-permute-start.24
  164.3 4.6 %collective-permute-done.22.other_ref = f32[1,256,512]{2,1,0:T(8,128)S(1)} collective-permute-done((f32[1,256,512]{2,1,0:T(8,128)S(1)}, f32[1,256,512]{2,1,0:T(8,128)S(1)}, u32[]{:S(2)}, u32[]{:S(2)}) %collective-permute-start.22) | collective-permute-done | bytes 524320 | tf_op jit(solution)/shard_map/ppermute | solution.py:1036
  172.6 1.6 collective-permute-start.28
  174.3 1.5 collective-permute-start.23
  175.7 5.4 %collective-permute-done.23.new_ref = f32[1,16,1664]{2,1,0:T(8,128)S(1)} collective-permute-done((f32[1,16,1664]{2,1,0:T(8,128)S(1)}, f32[1,16,1664]{2,1,0:T(8,128)S(1)}, u32[]{:S(2)}, u32[]{:S(2)}) %collective-permute-start.23) | collective-permute-done | bytes 106528 | tf_op jit(solution)/shard_map/ppermute | solution.py:1036
  185.5 5.7 %collective-permute-done.25.other_ref = f32[1,16,1664]{2,1,0:T(8,128)S(1)} collective-permute-done((f32[1,16,1664]{2,1,0:T(8,128)S(1)}, f32[1,16,1664]{2,1,0:T(8,128)S(1)}, u32[]{:S(2)}, u32[]{:S(2)}) %collective-permute-start.25) | collective-permute-done | bytes 106528 | tf_op jit(solution)/shard_map/ppermute | solution.py:1036
  191.8 2.3 collective-permute-done.29.other_ref
  194.7 2.1 collective-permute-start.31
  196.9 2.0 down_join1.1
  198.8 8.1 %collective-permute-done.27.other_ref = f32[1,32,1664]{2,1,0:T(8,128)S(1)} collective-permute-done((f32[1,32,1664]{2,1,0:T(8,128)S(1)}, f32[1,32,1664]{2,1,0:T(8,128)S(1)}, u32[]{:S(2)}, u32[]{:S(2)}) %collective-permute-start.27) | collective-permute-done | bytes 213024 | tf_op jit(solution)/shard_map/ppermute | solution.py:1036
  208.2 7.3 %shard_map.367 = (bf16[4,256,512]{2,1,0:T(8,128)(2,1)}, f32[8,128]{1,0:T(8,128)}) custom-call(s32[6]{0:T(128)} %stack.27.refs_1_.refs_0_.refs_2_.bits_ref, bf16[1024,2048]{1,0:T(8,128)(2,1)} %get-tuple-element.167.refs_1_, f32[4,256,512]{2,1,0:T(8,128)} %get-tuple-element.168.refs_4_.refs_2_, bf16[2048,512]{1,0:T(8,128)(2,1)} %refs_3_.5, f32[1,512]{1,0:T(1,128)} %bitcast.28, ...), custom_call_target="tpu_custom_call" | custom-call | flops 2147483648 | bytes 20000000 | tf_op jit(solution)/shard_map/pallas_call | solution.py:1238
  216.6 1.5 up_join1.1
  219.2 2.7 %collective-permute-start.32 = (f32[1,128,1664]{2,1,0:T(8,128)S(1)}, f32[1,128,1664]{2,1,0:T(8,128)S(1)}, u32[]{:S(2)}, u32[]{:S(2)}) collective-permute-start(f32[1,128,1664]{2,1,0:T(8,128)S(1)} %get-tuple-element.270.own_ref), channel_id=1, source_target_pairs={{0,8},{1,17},{2,10},{3,19},{4,12},{5,21},{6,14},{7,23},{8,0},{9,25... | collective-permute-start | bytes 2555912 | tf_op jit(solution)/shard_map/ppermute | solution.py:1036
  221.9 4.5 %down_place.1 = (f32[2048,512]{1,0:T(8,128)}, f32[8,128]{1,0:T(8,128)S(1)}) custom-call(s32[6]{0:T(128)S(1)} %copy-done.3, f32[1,1024,512]{2,1,0:T(8,128)} %get-tuple-element.271.own_ref, f32[1,1024,512]{2,1,0:T(8,128)} %collective-permute-done.33.other_ref, f32[8,128]{1,0:T(8,128)S(1)} %get-tuple-element.272.token_ref), custom_call_target="tpu_custom_call" | custom-call | bytes 40000000 | tf_op jit(solution)/shard_map/down_place/pallas_call | solution.py:1040
  226.4 6.1 %collective-permute-done.32.other_ref = f32[1,128,1664]{2,1,0:T(8,128)S(1)} collective-permute-done((f32[1,128,1664]{2,1,0:T(8,128)S(1)}, f32[1,128,1664]{2,1,0:T(8,128)S(1)}, u32[]{:S(2)}, u32[]{:S(2)}) %collective-permute-start.32) | collective-permute-done | bytes 852000 | tf_op jit(solution)/shard_map/ppermute | solution.py:1036
  233.3 3.2 %up_place.1 = (f32[512,2048]{1,0:T(8,128)}, f32[512,512]{1,0:T(8,128)}, f32[8,128]{1,0:T(8,128)S(1)}) custom-call(s32[6]{0:T(128)S(1)} %copy-done.3, f32[5,256,512]{2,1,0:T(8,128)S(1)} %get-tuple-element.275.own_ref, f32[5,256,512]{2,1,0:T(8,128)S(1)} %collective-permute-done.35.other_ref, f32[8,128]{1,0:T(8,128)S(1)} %get-tuple-element.276.token_ref), custom_call_target="tpu_custom_call" | custom-call | bytes 40000000 | tf_op jit(solution)/shard_map/up_place/pallas_call | solution.py:1040
  236.9 2.3 last_place.1
  (105 shorter events, 33.7 us)
Async XLA Ops:
  7.2 13.5 %collective-permute-start = (f32[4,16,1024]{2,1,0:T(8,128)}, f32[4,16,1024]{2,1,0:T(8,128)S(1)}, u32[]{:S(2)}, u32[]{:S(2)}) collective-permute-start(f32[4,16,1024]{2,1,0:T(8,128)} %get-tuple-element.162), channel_id=1, source_target_pairs={{0,8},{8,0},{16,24},{24,16},{1,9},{9,1},{17,25},{25,17},{2,10},{10... | collective-permute-start | bytes 786440 | tf_op jit(solution)/shard_map/ppermute | solution.py:1338
  10.1 10.5 %collective-permute-start.2 = (f32[4,8,1024]{2,1,0:T(8,128)}, f32[4,8,1024]{2,1,0:T(8,128)S(1)}, u32[]{:S(2)}, u32[]{:S(2)}) collective-permute-start(f32[4,8,1024]{2,1,0:T(8,128)} %get-tuple-element.163), channel_id=1, source_target_pairs={{0,24},{8,16},{16,8},{24,0},{1,25},{9,17},{17,9},{25,1},{2,26},{10... | collective-permute-start | bytes 393224 | tf_op jit(solution)/shard_map/ppermute | solution.py:1338
  11.6 9.0 %collective-permute-start.1 = (f32[4,8,1024]{2,1,0:T(8,128)}, f32[4,8,1024]{2,1,0:T(8,128)S(1)}, u32[]{:S(2)}, u32[]{:S(2)}) collective-permute-start(f32[4,8,1024]{2,1,0:T(8,128)} %get-tuple-element.163), channel_id=1, source_target_pairs={{0,16},{8,24},{16,0},{24,8},{1,17},{9,25},{17,1},{25,9},{2,18},{10... | collective-permute-start | bytes 393224 | tf_op jit(solution)/shard_map/ppermute | solution.py:1338
  20.7 0.7 copy-start.16
  20.7 0.8 copy-start.13
  49.9 14.9 %collective-permute-start.3 = (f32[1,1024,512]{2,1,0:T(8,128)}, f32[1,1024,512]{2,1,0:T(8,128)}, u32[]{:S(2)}, u32[]{:S(2)}) collective-permute-start(f32[1,1024,512]{2,1,0:T(8,128)} %get-tuple-element.184), channel_id=1, source_target_pairs={{0,1},{1,0},{2,3},{3,2},{4,5},{5,4},{6,7},{7,6},{8,9},{9,8},{10,11... | collective-permute-start | bytes 6291464 | tf_op jit(solution)/shard_map/ppermute | solution.py:1036
  60.7 15.4 %collective-permute-start.4 = (f32[5,256,512]{2,1,0:T(8,128)}, f32[5,256,512]{2,1,0:T(8,128)}, u32[]{:S(2)}, u32[]{:S(2)}) collective-permute-start(f32[5,256,512]{2,1,0:T(8,128)} %get-tuple-element.190), channel_id=1, source_target_pairs={{0,1},{1,0},{2,3},{3,2},{4,5},{5,4},{6,7},{7,6},{8,9},{9,8},{10,11... | collective-permute-start | bytes 7864328 | tf_op jit(solution)/shard_map/ppermute | solution.py:1036
  61.3 12.5 %collective-permute-start.5 = (f32[4,16,1024]{2,1,0:T(8,128)}, f32[4,16,1024]{2,1,0:T(8,128)S(1)}, u32[]{:S(2)}, u32[]{:S(2)}) collective-permute-start(f32[4,16,1024]{2,1,0:T(8,128)} %get-tuple-element.192), channel_id=1, source_target_pairs={{0,8},{8,0},{16,24},{24,16},{1,9},{9,1},{17,25},{25,17},{2,10},{10... | collective-permute-start | bytes 786440 | tf_op jit(solution)/shard_map/ppermute | solution.py:1338
  62.8 11.0 %collective-permute-start.6 = (f32[4,8,1024]{2,1,0:T(8,128)}, f32[4,8,1024]{2,1,0:T(8,128)S(1)}, u32[]{:S(2)}, u32[]{:S(2)}) collective-permute-start(f32[4,8,1024]{2,1,0:T(8,128)} %get-tuple-element.193), channel_id=1, source_target_pairs={{0,16},{8,24},{16,0},{24,8},{1,17},{9,25},{17,1},{25,9},{2,18},{10... | collective-permute-start | bytes 393224 | tf_op jit(solution)/shard_map/ppermute | solution.py:1338
  64.3 9.5 %collective-permute-start.7 = (f32[4,8,1024]{2,1,0:T(8,128)}, f32[4,8,1024]{2,1,0:T(8,128)S(1)}, u32[]{:S(2)}, u32[]{:S(2)}) collective-permute-start(f32[4,8,1024]{2,1,0:T(8,128)} %get-tuple-element.194), channel_id=1, source_target_pairs={{0,24},{8,16},{16,8},{24,0},{1,25},{9,17},{17,9},{25,1},{2,26},{10... | collective-permute-start | bytes 393224 | tf_op jit(solution)/shard_map/ppermute | solution.py:1338
  73.8 0.7 copy-start.19
  73.8 0.8 copy-start.17
  74.6 15.0 %collective-permute-start.8 = (f32[1,512,512]{2,1,0:T(8,128)}, f32[1,512,512]{2,1,0:T(8,128)S(1)}, u32[]{:S(2)}, u32[]{:S(2)}) collective-permute-start(f32[1,512,512]{2,1,0:T(8,128)} %get-tuple-element.206), channel_id=1, source_target_pairs={{0,8},{1,17},{2,10},{3,19},{4,12},{5,21},{6,14},{7,23},{8,0},{9,25... | collective-permute-start | bytes 3145736 | tf_op jit(solution)/shard_map/ppermute | solution.py:1036
  84.7 26.8 %collective-permute-start.11 = (f32[5,128,512]{2,1,0:T(8,128)}, f32[5,128,512]{2,1,0:T(8,128)}, u32[]{:S(2)}, u32[]{:S(2)}) collective-permute-start(f32[5,128,512]{2,1,0:T(8,128)} %get-tuple-element.216), channel_id=1, source_target_pairs={{0,8},{1,17},{2,10},{3,19},{4,12},{5,21},{6,14},{7,23},{8,0},{9,25... | collective-permute-start | bytes 3932168 | tf_op jit(solution)/shard_map/ppermute | solution.py:1036
  89.6 1.0 copy-start.14
  94.5 13.5 %collective-permute-start.9 = (f32[1,256,512]{2,1,0:T(8,128)}, f32[1,256,512]{2,1,0:T(8,128)S(1)}, u32[]{:S(2)}, u32[]{:S(2)}) collective-permute-start(f32[1,256,512]{2,1,0:T(8,128)} %get-tuple-element.212), channel_id=1, source_target_pairs={{0,16},{1,9},{2,18},{3,11},{4,20},{5,13},{6,22},{7,15},{8,24},{9,1... | collective-permute-start | bytes 1572872 | tf_op jit(solution)/shard_map/ppermute | solution.py:1036
  96.0 12.0 %copy-start.1 = (s32[6]{0:T(128)S(1)}, s32[6]{0:T(128)}, u32[]{:S(2)}) copy-start(s32[6]{0:T(128)} %stack.27.refs_1_.refs_0_.refs_2_.bits_ref) | copy-start | bytes 76
  96.0 12.0 %copy-start.5 = (f32[1,256,512]{2,1,0:T(8,128)S(1)}, f32[1,256,512]{2,1,0:T(8,128)}, u32[]{:S(2)}) copy-start(f32[1,256,512]{2,1,0:T(8,128)} %get-tuple-element.211.keep_ref) | copy-start | bytes 1572868
  108.1 0.7 copy-start.6
  110.0 7.6 %collective-permute-start.10 = (f32[1,128,512]{2,1,0:T(8,128)S(1)}, f32[1,128,512]{2,1,0:T(8,128)S(1)}, u32[]{:S(2)}, u32[]{:S(2)}) collective-permute-start(f32[1,128,512]{2,1,0:T(8,128)S(1)} %get-tuple-element.215), channel_id=1, source_target_pairs={{0,2},{1,5},{2,0},{3,7},{4,6},{5,1},{6,4},{7,3},{8,10},{9,13},{10,... | collective-permute-start | bytes 786440 | tf_op jit(solution)/shard_map/ppermute | solution.py:1036
  111.5 6.0 %copy-start.2 = (s32[6]{0:T(128)S(1)}, s32[6]{0:T(128)}, u32[]{:S(2)}) copy-start(s32[6]{0:T(128)} %stack.27.refs_1_.refs_0_.refs_2_.bits_ref) | copy-start | bytes 76
  115.8 12.8 %copy-start = (f32[1,256,1664]{2,1,0:T(8,128)S(1)}, f32[1,256,1664]{2,1,0:T(8,128)}, u32[]{:S(2)}) copy-start(f32[1,256,1664]{2,1,0:T(8,128)} %get-tuple-element.209.keep_ref) | copy-start | bytes 5111812
  119.4 11.7 %copy-start.4 = (f32[5,64,512]{2,1,0:T(8,128)S(1)}, f32[5,64,512]{2,1,0:T(8,128)}, u32[]{:S(2)}) copy-start(f32[5,64,512]{2,1,0:T(8,128)} %get-tuple-element.227.keep_ref) | copy-start | bytes 1966084
  119.4 9.3 %collective-permute-start.12 = (f32[1,256,1664]{2,1,0:T(8,128)}, f32[1,256,1664]{2,1,0:T(8,128)S(1)}, u32[]{:S(2)}, u32[]{:S(2)}) collective-permute-start(f32[1,256,1664]{2,1,0:T(8,128)} %get-tuple-element.220), channel_id=1, source_target_pairs={{0,1},{1,0},{2,3},{3,2},{4,5},{5,4},{6,7},{7,6},{8,9},{9,8},{10,11... | collective-permute-start | bytes 5111816 | tf_op jit(solution)/shard_map/ppermute | solution.py:1036
  120.0 11.1 %collective-permute-start.16 = (f32[5,64,512]{2,1,0:T(8,128)}, f32[5,64,512]{2,1,0:T(8,128)S(1)}, u32[]{:S(2)}, u32[]{:S(2)}) collective-permute-start(f32[5,64,512]{2,1,0:T(8,128)} %get-tuple-element.228), channel_id=1, source_target_pairs={{0,16},{1,9},{2,18},{3,11},{4,20},{5,13},{6,22},{7,15},{8,24},{9,1... | collective-permute-start | bytes 1966088 | tf_op jit(solution)/shard_map/ppermute | solution.py:1036
  121.5 6.0 %collective-permute-start.13 = (f32[1,64,512]{2,1,0:T(8,128)S(1)}, f32[1,64,512]{2,1,0:T(8,128)S(1)}, u32[]{:S(2)}, u32[]{:S(2)}) collective-permute-start(f32[1,64,512]{2,1,0:T(8,128)S(1)} %get-tuple-element.222), channel_id=1, source_target_pairs={{0,4},{1,3},{2,6},{3,1},{4,0},{5,7},{6,2},{7,5},{8,12},{9,11},{10,... | collective-permute-start | bytes 393224 | tf_op jit(solution)/shard_map/ppermute | solution.py:1036
  129.5 16.5 %collective-permute-start.14 = (f32[1,128,1664]{2,1,0:T(8,128)S(1)}, f32[1,128,1664]{2,1,0:T(8,128)S(1)}, u32[]{:S(2)}, u32[]{:S(2)}) collective-permute-start(f32[1,128,1664]{2,1,0:T(8,128)S(1)} %get-tuple-element.225), channel_id=1, source_target_pairs={{0,8},{1,17},{2,10},{3,19},{4,12},{5,21},{6,14},{7,23},{8,0},{9,25... | collective-permute-start | bytes 2555912 | tf_op jit(solution)/shard_map/ppermute | solution.py:1036
  131.7 13.1 %collective-permute-start.17 = (f32[5,32,512]{2,1,0:T(8,128)S(1)}, f32[5,32,512]{2,1,0:T(8,128)S(1)}, u32[]{:S(2)}, u32[]{:S(2)}) collective-permute-start(f32[5,32,512]{2,1,0:T(8,128)S(1)} %get-tuple-element.231), channel_id=1, source_target_pairs={{0,2},{1,5},{2,0},{3,7},{4,6},{5,1},{6,4},{7,3},{8,10},{9,13},{10,... | collective-permute-start | bytes 983048 | tf_op jit(solution)/shard_map/ppermute | solution.py:1036
  133.8 11.6 %collective-permute-start.15 = (f32[1,64,512]{2,1,0:T(8,128)S(1)}, f32[1,64,512]{2,1,0:T(8,128)S(1)}, u32[]{:S(2)}, u32[]{:S(2)}) collective-permute-start(f32[1,64,512]{2,1,0:T(8,128)S(1)} %get-tuple-element.226.own_ref), channel_id=1, source_target_pairs={{0,4},{1,3},{2,6},{3,1},{4,0},{5,7},{6,2},{7,5},{8,12},{9,11},{10,... | collective-permute-start | bytes 393224 | tf_op jit(solution)/shard_map/ppermute | solution.py:1036
  146.9 8.2 %collective-permute-start.18 = (f32[1,64,1664]{2,1,0:T(8,128)S(1)}, f32[1,64,1664]{2,1,0:T(8,128)S(1)}, u32[]{:S(2)}, u32[]{:S(2)}) collective-permute-start(f32[1,64,1664]{2,1,0:T(8,128)S(1)} %get-tuple-element.236), channel_id=1, source_target_pairs={{0,16},{1,9},{2,18},{3,11},{4,20},{5,13},{6,22},{7,15},{8,24},{9,1... | collective-permute-start | bytes 1277960 | tf_op jit(solution)/shard_map/ppermute | solution.py:1036
  147.9 11.2 %collective-permute-start.20 = (f32[1,128,512]{2,1,0:T(8,128)S(1)}, f32[1,128,512]{2,1,0:T(8,128)S(1)}, u32[]{:S(2)}, u32[]{:S(2)}) collective-permute-start(f32[1,128,512]{2,1,0:T(8,128)S(1)} %get-tuple-element.240.own_ref), channel_id=1, source_target_pairs={{0,2},{1,5},{2,0},{3,7},{4,6},{5,1},{6,4},{7,3},{8,10},{9,13},{10,... | collective-permute-start | bytes 786440 | tf_op jit(solution)/shard_map/ppermute | solution.py:1036
  149.4 7.8 %collective-permute-start.21 = (f32[5,16,512]{2,1,0:T(8,128)S(1)}, f32[5,16,512]{2,1,0:T(8,128)S(1)}, u32[]{:S(2)}, u32[]{:S(2)}) collective-permute-start(f32[5,16,512]{2,1,0:T(8,128)S(1)} %get-tuple-element.242), channel_id=1, source_target_pairs={{0,4},{1,3},{2,6},{3,1},{4,0},{5,7},{6,2},{7,5},{8,12},{9,11},{10,... | collective-permute-start | bytes 491528 | tf_op jit(solution)/shard_map/ppermute | solution.py:1036
  159.7 9.2 %collective-permute-start.22 = (f32[1,256,512]{2,1,0:T(8,128)S(1)}, f32[1,256,512]{2,1,0:T(8,128)S(1)}, u32[]{:S(2)}, u32[]{:S(2)}) collective-permute-start(f32[1,256,512]{2,1,0:T(8,128)S(1)} %get-tuple-element.245.own_ref), channel_id=1, source_target_pairs={{0,16},{1,9},{2,18},{3,11},{4,20},{5,13},{6,22},{7,15},{8,24},{9,1... | collective-permute-start | bytes 1572872 | tf_op jit(solution)/shard_map/ppermute | solution.py:1036
  161.2 8.9 %collective-permute-start.19 = (f32[1,32,1664]{2,1,0:T(8,128)S(1)}, f32[1,32,1664]{2,1,0:T(8,128)S(1)}, u32[]{:S(2)}, u32[]{:S(2)}) collective-permute-start(f32[1,32,1664]{2,1,0:T(8,128)S(1)} %get-tuple-element.239), channel_id=1, source_target_pairs={{0,2},{1,5},{2,0},{3,7},{4,6},{5,1},{6,4},{7,3},{8,10},{9,13},{10,... | collective-permute-start | bytes 638984 | tf_op jit(solution)/shard_map/ppermute | solution.py:1036
  162.6 8.1 %collective-permute-start.24 = (f32[5,16,512]{2,1,0:T(8,128)S(1)}, f32[5,16,512]{2,1,0:T(8,128)S(1)}, u32[]{:S(2)}, u32[]{:S(2)}) collective-permute-start(f32[5,16,512]{2,1,0:T(8,128)S(1)} %get-tuple-element.250.own_ref), channel_id=1, source_target_pairs={{0,4},{1,3},{2,6},{3,1},{4,0},{5,7},{6,2},{7,5},{8,12},{9,11},{10,... | collective-permute-start | bytes 491528 | tf_op jit(solution)/shard_map/ppermute | solution.py:1036
  171.3 11.6 %collective-permute-start.26 = (f32[5,32,512]{2,1,0:T(8,128)S(1)}, f32[5,32,512]{2,1,0:T(8,128)S(1)}, u32[]{:S(2)}, u32[]{:S(2)}) collective-permute-start(f32[5,32,512]{2,1,0:T(8,128)S(1)} %get-tuple-element.254.own_ref), channel_id=1, source_target_pairs={{0,2},{1,5},{2,0},{3,7},{4,6},{5,1},{6,4},{7,3},{8,10},{9,13},{10,... | collective-permute-start | bytes 983048 | tf_op jit(solution)/shard_map/ppermute | solution.py:1036
  172.6 24.2 %collective-permute-start.28 = (f32[1,512,512]{2,1,0:T(8,128)S(1)}, f32[1,512,512]{2,1,0:T(8,128)S(1)}, u32[]{:S(2)}, u32[]{:S(2)}) collective-permute-start(f32[1,512,512]{2,1,0:T(8,128)S(1)} %get-tuple-element.258.own_ref), channel_id=1, source_target_pairs={{0,8},{1,17},{2,10},{3,19},{4,12},{5,21},{6,14},{7,23},{8,0},{9,25... | collective-permute-start | bytes 3145736 | tf_op jit(solution)/shard_map/ppermute | solution.py:1036
  174.3 6.9 %collective-permute-start.23 = (f32[1,16,1664]{2,1,0:T(8,128)S(1)}, f32[1,16,1664]{2,1,0:T(8,128)S(1)}, u32[]{:S(2)}, u32[]{:S(2)}) collective-permute-start(f32[1,16,1664]{2,1,0:T(8,128)S(1)} %get-tuple-element.249), channel_id=1, source_target_pairs={{0,4},{1,3},{2,6},{3,1},{4,0},{5,7},{6,2},{7,5},{8,12},{9,11},{10,... | collective-permute-start | bytes 319496 | tf_op jit(solution)/shard_map/ppermute | solution.py:1036
  183.4 10.7 %collective-permute-start.29 = (f32[5,64,512]{2,1,0:T(8,128)S(1)}, f32[5,64,512]{2,1,0:T(8,128)S(1)}, u32[]{:S(2)}, u32[]{:S(2)}) collective-permute-start(f32[5,64,512]{2,1,0:T(8,128)S(1)} %get-tuple-element.259.own_ref), channel_id=1, source_target_pairs={{0,16},{1,9},{2,18},{3,11},{4,20},{5,13},{6,22},{7,15},{8,24},{9,1... | collective-permute-start | bytes 1966088 | tf_op jit(solution)/shard_map/ppermute | solution.py:1036
  184.8 6.5 %collective-permute-start.25 = (f32[1,16,1664]{2,1,0:T(8,128)S(1)}, f32[1,16,1664]{2,1,0:T(8,128)S(1)}, u32[]{:S(2)}, u32[]{:S(2)}) collective-permute-start(f32[1,16,1664]{2,1,0:T(8,128)S(1)} %get-tuple-element.253.own_ref), channel_id=1, source_target_pairs={{0,4},{1,3},{2,6},{3,1},{4,0},{5,7},{6,2},{7,5},{8,12},{9,11},{10,... | collective-permute-start | bytes 319496 | tf_op jit(solution)/shard_map/ppermute | solution.py:1036
  194.7 21.1 %collective-permute-start.31 = (f32[5,128,512]{2,1,0:T(8,128)S(1)}, f32[5,128,512]{2,1,0:T(8,128)}, u32[]{:S(2)}, u32[]{:S(2)}) collective-permute-start(f32[5,128,512]{2,1,0:T(8,128)S(1)} %get-tuple-element.267.own_ref), channel_id=1, source_target_pairs={{0,8},{1,17},{2,10},{3,19},{4,12},{5,21},{6,14},{7,23},{8,0},{9,25... | collective-permute-start | bytes 3932168 | tf_op jit(solution)/shard_map/ppermute | solution.py:1036
  198.8 23.0 %collective-permute-start.33 = (f32[1,1024,512]{2,1,0:T(8,128)}, f32[1,1024,512]{2,1,0:T(8,128)}, u32[]{:S(2)}, u32[]{:S(2)}) collective-permute-start(f32[1,1024,512]{2,1,0:T(8,128)} %get-tuple-element.271.own_ref), channel_id=1, source_target_pairs={{0,1},{1,0},{2,3},{3,2},{4,5},{5,4},{6,7},{7,6},{8,9},{9,8},{10,11... | collective-permute-start | bytes 6291464 | tf_op jit(solution)/shard_map/ppermute | solution.py:1036
  198.8 8.1 %collective-permute-start.27 = (f32[1,32,1664]{2,1,0:T(8,128)S(1)}, f32[1,32,1664]{2,1,0:T(8,128)S(1)}, u32[]{:S(2)}, u32[]{:S(2)}) collective-permute-start(f32[1,32,1664]{2,1,0:T(8,128)S(1)} %get-tuple-element.257.own_ref), channel_id=1, source_target_pairs={{0,2},{1,5},{2,0},{3,7},{4,6},{5,1},{6,4},{7,3},{8,10},{9,13},{10,... | collective-permute-start | bytes 638984 | tf_op jit(solution)/shard_map/ppermute | solution.py:1036
  207.6 10.6 %collective-permute-start.30 = (f32[1,64,1664]{2,1,0:T(8,128)S(1)}, f32[1,64,1664]{2,1,0:T(8,128)}, u32[]{:S(2)}, u32[]{:S(2)}) collective-permute-start(f32[1,64,1664]{2,1,0:T(8,128)S(1)} %get-tuple-element.266.own_ref), channel_id=1, source_target_pairs={{0,16},{1,9},{2,18},{3,11},{4,20},{5,13},{6,22},{7,15},{8,24},{9,1... | collective-permute-start | bytes 1277960 | tf_op jit(solution)/shard_map/ppermute | solution.py:1036
  208.1 7.7 %copy-start.3 = (s32[6]{0:T(128)S(1)}, s32[6]{0:T(128)}, u32[]{:S(2)}) copy-start(s32[6]{0:T(128)} %stack.27.refs_1_.refs_0_.refs_2_.bits_ref) | copy-start | bytes 76
  218.1 15.2 %collective-permute-start.35 = (f32[5,256,512]{2,1,0:T(8,128)S(1)}, f32[5,256,512]{2,1,0:T(8,128)S(1)}, u32[]{:S(2)}, u32[]{:S(2)}) collective-permute-start(f32[5,256,512]{2,1,0:T(8,128)S(1)} %get-tuple-element.275.own_ref), channel_id=1, source_target_pairs={{0,1},{1,0},{2,3},{3,2},{4,5},{5,4},{6,7},{7,6},{8,9},{9,8},{10,11... | collective-permute-start | bytes 7864328 | tf_op jit(solution)/shard_map/ppermute | solution.py:1036
  219.2 13.3 %collective-permute-start.32 = (f32[1,128,1664]{2,1,0:T(8,128)S(1)}, f32[1,128,1664]{2,1,0:T(8,128)S(1)}, u32[]{:S(2)}, u32[]{:S(2)}) collective-permute-start(f32[1,128,1664]{2,1,0:T(8,128)S(1)} %get-tuple-element.270.own_ref), channel_id=1, source_target_pairs={{0,8},{1,17},{2,10},{3,19},{4,12},{5,21},{6,14},{7,23},{8,0},{9,25... | collective-permute-start | bytes 2555912 | tf_op jit(solution)/shard_map/ppermute | solution.py:1036
  233.2 3.7 %collective-permute-start.34 = (f32[1,256,1664]{2,1,0:T(8,128)S(1)}, f32[1,256,1664]{2,1,0:T(8,128)S(1)}, u32[]{:S(2)}, u32[]{:S(2)}) collective-permute-start(f32[1,256,1664]{2,1,0:T(8,128)S(1)} %get-tuple-element.274.own_ref), channel_id=1, source_target_pairs={{0,1},{1,0},{2,3},{3,2},{4,5},{5,4},{6,7},{7,6},{8,9},{9,8},{10,11... | collective-permute-start | bytes 5111816 | tf_op jit(solution)/shard_map/ppermute | solution.py:1036
  (8 other events, 5.2 us)
